TPU v7x, 512 devices: a whole 4x8x8 slice. The times are simulated.
512 devices in a mesh: dp: 128 (over x, y_lo, z, core), mp: 4 (over y_hi).
Axes of the slice: x: 4, y: 8 (y_hi: 4, y_lo: 2; y = y_hi * 2 + y_lo), z: 8, core: 2. Of those that a mesh axis runs over, the one named last changes fastest.
Arguments:
- images: bfloat16 [256, 256, 3136], P('dp', 'mp'), may hold values from -16 to 16
- permutation: int32 [256], replicated, may hold values from 0 to 255, as said below
- inverse: int32 [256], replicated, may hold values from 0 to 255, as said below
- reduce_weight: bfloat16 [64, 256], P(None, 'mp'), may hold values from -0.375 to 0.375
- reduce_gain: float32 [64], P('mp'), may hold values from 0.5 to 1.5
- reduce_shift: float32 [64], P('mp'), may hold values from -3 to 3
- spatial_weight: bfloat16 [64, 64, 3, 3], P('mp'), may hold values from -0.25 to 0.25
- spatial_gain: float32 [64], P('mp'), may hold values from 0.5 to 1.5
- spatial_shift: float32 [64], P('mp'), may hold values from -3 to 3
- expand_weight: bfloat16 [256, 64], P('mp'), may hold values from -0.75 to 0.75
- expand_gain: float32 [256], P('mp'), may hold values from 0.5 to 1.5
- expand_shift: float32 [256], P('mp'), may hold values from -3 to 3
- projection: bfloat16 [256, 128], P('mp'), may hold values from -0.375 to 0.375
- queries: float32 [256, 128], P('dp'), may hold values from -6 to 6
- dictionary_bank: bfloat16 [4096, 128], P('mp'), may hold values from -1.5 to 1.5
Outputs:
- features: bfloat16 [256, 256, 3136], P('dp', 'mp')
- matched_similarity_scores: float32 [256, 256], P('dp')
- loss: float32 [256], P('dp')
Inputs may be any that keep to these rules, and one draw needn't show every extreme that they name: A permutation: every value of 0 to 255 once. The inverse of permutation: inverse[permutation[i]] = i.
All inputs are finite; a program needn't handle non-finite values.
Results may differ from a plain program's by a relative error of at most 0.015.
Values may be sent and summed in bfloat16 or wider, within the bound.
A program may use at most 64 MiB of HBM per device.

v0:
```python
import jax
import jax.numpy as jnp
from jax import lax
from jax.sharding import PartitionSpec as P

SIDE = 56


sharpness_divisor = 0.2


def normalize(values, gain_vec, shift_vec):
    center = jnp.mean(values, axis=(0, 2), keepdims=True)
    spread = jnp.mean((values - center) ** 2, axis=(0, 2), keepdims=True)
    return (values - center) * lax.rsqrt(spread + 1e-05) * gain_vec[None, :, None] + shift_vec[
        None, :, None
    ]


def reshuffle_pictures(section, ordering):
    batch, channels, picture_elements = section.shape
    groups = lax.axis_size("dp")
    tensor_arrangement = section.reshape(batch, groups, channels * picture_elements // groups)
    columns = lax.all_to_all(tensor_arrangement, "dp", split_axis=1, concat_axis=0, tiled=True)
    columns = jnp.take(columns.reshape(batch * groups, -1), ordering, axis=0)
    arrived = lax.all_to_all(
        columns.reshape(batch * groups, 1, -1), "dp", split_axis=0, concat_axis=1, tiled=True
    )
    return arrived.reshape(batch, channels, picture_elements)


def restore_images(section, ordering):
    batch, channels, picture_elements = section.shape
    groups = lax.axis_size("dp")
    tensor_arrangement = section.reshape(batch, groups, channels * picture_elements // groups)
    columns = lax.all_to_all(tensor_arrangement, "dp", split_axis=1, concat_axis=0, tiled=True)
    columns = jnp.take(columns.reshape(batch * groups, -1), ordering, axis=0)
    arrived = lax.all_to_all(
        columns.reshape(batch * groups, 1, -1), "dp", split_axis=0, concat_axis=1, tiled=True
    )
    return arrived.reshape(batch, channels, picture_elements)


def on_device(
    images,
    permutation,
    inverse,
    reduce_weight,
    reduce_gain,
    reduce_shift,
    spatial_weight,
    spatial_gain,
    spatial_shift,
    expand_weight,
    expand_gain,
    expand_shift,
    projection,
    queries,
    dictionary_bank,
):
    batch = images.shape[0]
    picture_elements = images.shape[2]
    partial_sums = jnp.einsum(
        "oc,bcp->bop",
        reduce_weight,
        reshuffle_pictures(images, permutation),
        preferred_element_type=jnp.float32,
    )
    shuffled = lax.psum_scatter(
        partial_sums.astype(jnp.bfloat16), "mp", scatter_dimension=1, tiled=True
    )
    first = jnp.maximum(
        normalize(shuffled.astype(jnp.float32), reduce_gain, reduce_shift), 0.0
    ).astype(jnp.bfloat16)
    spatial_init = jnp.zeros((batch, spatial_weight.shape[0], picture_elements), jnp.float32)
    portion = lax.all_gather(first, "mp", axis=1, tiled=True)
    width = portion.shape[1]
    kernel = spatial_weight
    maps = portion.reshape(batch, width, SIDE, SIDE)
    result = lax.conv_general_dilated(
        maps,
        kernel,
        (1, 1),
        "SAME",
        dimension_numbers=("NCHW", "OIHW", "NCHW"),
        preferred_element_type=jnp.float32,
    )
    spatial = spatial_init + result.reshape(batch, -1, picture_elements)
    second = jnp.maximum(normalize(spatial, spatial_gain, spatial_shift), 0.0).astype(jnp.bfloat16)
    expand_init = jnp.zeros((batch, expand_weight.shape[0], picture_elements), jnp.float32)
    portion = lax.all_gather(second, "mp", axis=1, tiled=True)
    kernel = lax.slice_in_dim(expand_weight, 0, portion.shape[1], axis=1)
    expanded = expand_init + jnp.einsum(
        "om,bmp->bop", kernel, portion, preferred_element_type=jnp.float32
    )
    third = normalize(expanded, expand_gain, expand_shift).astype(jnp.bfloat16)
    restored = restore_images(third, inverse)
    features = jnp.maximum(restored.astype(jnp.float32) + images.astype(jnp.float32), 0.0).astype(
        jnp.bfloat16
    )
    pooled = jnp.mean(features.astype(jnp.float32), axis=2)
    partial_embed = jnp.dot(pooled, projection.astype(jnp.float32), precision=lax.Precision.HIGHEST)
    embedded = lax.psum(partial_embed, "mp")
    momentum_embeddings_out = (
        embedded * lax.rsqrt(jnp.sum(embedded * embedded, axis=1, keepdims=True) + 1e-06)
    ).astype(jnp.bfloat16)
    unit_length_probes = (
        queries * lax.rsqrt(jnp.sum(queries * queries, axis=1, keepdims=True) + 1e-06)
    ).astype(jnp.bfloat16)
    own_logits = (
        jnp.sum(
            unit_length_probes.astype(jnp.float32) * momentum_embeddings_out.astype(jnp.float32),
            axis=1,
        )
        / sharpness_divisor
    )
    matched_similarity_scores = (
        jnp.einsum(
            "qe,ke->qk",
            unit_length_probes,
            lax.all_gather(momentum_embeddings_out, "dp", axis=0, tiled=True),
            preferred_element_type=jnp.float32,
        )
        / sharpness_divisor
    )
    stored_similarity_scores = (
        jnp.einsum(
            "qe,ke->qk", unit_length_probes, dictionary_bank, preferred_element_type=jnp.float32
        )
        / sharpness_divisor
    )
    queue_part = jnp.sum(jnp.exp(stored_similarity_scores), axis=1)
    queue_mass = lax.psum(queue_part, "mp")
    loss = jnp.log(jnp.sum(jnp.exp(matched_similarity_scores), axis=1) + queue_mass) - own_logits
    return (features, matched_similarity_scores, loss)


def solution(mesh):
    placed = (
        P("dp", "mp", None),
        P(),
        P(),
        P(None, "mp"),
        P("mp"),
        P("mp"),
        P("mp", None, None, None),
        P("mp"),
        P("mp"),
        P("mp", None),
        P("mp"),
        P("mp"),
        P("mp", None),
        P("dp", None),
        P("mp", None),
    )
    return jax.shard_map(
        on_device,
        mesh=mesh,
        in_specs=placed,
        out_specs=(P("dp", "mp", None), P("dp", None), P("dp")),
        check_vma=False,
    )
```

profile of v0, /device:TPU:1, one launch (start us, length us, event | category | flops | bytes accessed | tf_op | source)
XLA Modules:
  0.0 446.7 jit_solution(10245023574631335256)
XLA Ops:
  7.2 1.8 reshape.101
  9.0 1.8 copy.32
  10.8 16.6 %all-to-all-start = ((bf16[2,128,1568]{2,0,1:T(2,128)(2,1)}), bf16[2,128,1568]{2,0,1:T(2,128)(2,1)S(1)}, u32[]{:S(2)}, u32[]{:S(2)}) async-start(bf16[2,128,1568]{2,0,1:T(2,128)(2,1)} %copy.32), calls=%async_computation | async-start | bytes 1703936 | tf_op jit(solution)/shard_map/all_to_all | solution.py:24
  27.5 23.6 %all-to-all-done = bf16[2,128,1568]{2,0,1:T(2,128)(2,1)S(1)} async-done(((bf16[2,128,1568]{2,0,1:T(2,128)(2,1)}), bf16[2,128,1568]{2,0,1:T(2,128)(2,1)S(1)}, u32[]{:S(2)}, u32[]{:S(2)}) %all-to-all-start) | async-done | bytes 802848 | tf_op jit(solution)/shard_map/all_to_all | solution.py:24
  51.8 1.4 gather_fusion
  53.9 1.2 reduce.5
  55.5 32.5 %all_to_all.54 = bf16[128,2,1568]{2,1,0:T(2,128)(2,1)S(1)} all-to-all(bf16[128,2,1568]{2,1,0:T(2,128)(2,1)S(1)} %reshape.151), channel_id=1, replica_groups=mesh['dp'=128,'mp'=4] {'dp'}, dimensions={0} | all-to-all | bytes 1605632 | tf_op jit(solution)/shard_map/all_to_all | solution.py:26
  88.8 5.4 %reduce.4 = bf16[256,1568]{1,0:T(8,128)(2,1)S(1)} reduce(bf16[256,1,1568]{2,1,0:T(2,128)(2,1)S(1)} %reshape.152, bf16[]{:T(256)} %constant.49), dimensions={1}, to_apply=%all_to_all.43.reduce_sub_computation | reduce | bytes 1605634 | tf_op jit(solution)/shard_map/all_to_all | solution.py:26
  95.3 1.2 fusion.1
  96.6 29.4 %reduce-scatter.2.cloned.1.call-done = bf16[2,16,3136]{2,1,0:T(8,128)(2,1)} async-done(((bf16[2,64,3136]{2,1,0:T(8,128)(2,1)}), bf16[2,16,3136]{2,1,0:T(8,128)(2,1)}) %reduce-scatter.2.cloned.1.call-update) | async-done | bytes 200720 | tf_op jit(solution)/shard_map/reduce_scatter | solution.py:69
  129.3 17.0 %all_gather.9 = bf16[2,64,3136]{2,1,0:T(8,128)(2,1)S(1)} all-gather(bf16[2,16,3136]{2,1,0:T(8,128)(2,1)S(1)} %fusion.17), channel_id=1, replica_groups=mesh['dp'=128,'mp'=4] {'mp'}, dimensions={1}, use_global_device_ids=true | all-gather | bytes 1003520 | tf_op jit(solution)/shard_map/all_gather | solution.py:76
  146.3 1.9 reshape.105
  148.2 2.7 copy.43
  150.9 2.1 pad_bitcast_fusion
  153.3 1.2 fusion.2
  154.5 6.2 %select_reduce_fusion.1 = (f32[16]{0:T(128)S(1)}, f32[56,16,8,16]{3,1,2,0:T(8,128)}) fusion(pred[16,8]{0,1:T(8,128)(4,1)S(1)} %copy-done.5, bf16[16,64,3,3]{1,0,3,2:T(8,128)(2,1)S(1)} %copy-done.15, bf16[64,56,2,8,10]{0,4,3,2,1:T(8,128)(2,1)S(1)} %fusion.2), kind=kOutput, calls=%fused_computation.8 | convolution fusion | flops 130891760 | bytes 1624256 | tf_op jit(solution)/shard_map/conv_general_dilated | solution.py:80
  160.7 3.3 copy.37
  164.0 3.1 select_reduce_fusion
  168.1 13.7 %all_gather.10 = bf16[2,64,3136]{2,1,0:T(8,128)(2,1)S(1)} all-gather(bf16[2,16,3136]{2,1,0:T(8,128)(2,1)S(1)} %maximum_convert_fusion.1), channel_id=1, replica_groups=mesh['dp'=128,'mp'=4] {'mp'}, dimensions={1}, use_global_device_ids=true | all-gather | bytes 1003520 | tf_op jit(solution)/shard_map/all_gather | solution.py:91
  183.5 1.8 copy.39
  185.2 21.6 %all-to-all-start.2 = ((bf16[2,128,1568]{2,0,1:T(2,128)(2,1)}), bf16[2,128,1568]{2,0,1:T(2,128)(2,1)S(1)}, u32[]{:S(2)}, u32[]{:S(2)}) async-start(bf16[2,128,1568]{2,0,1:T(2,128)(2,1)} %copy.39), calls=%async_computation.3 | async-start | bytes 1703936 | tf_op jit(solution)/shard_map/all_to_all | solution.py:36
  206.9 23.7 %all-to-all-done.2 = bf16[2,128,1568]{2,0,1:T(2,128)(2,1)S(1)} async-done(((bf16[2,128,1568]{2,0,1:T(2,128)(2,1)}), bf16[2,128,1568]{2,0,1:T(2,128)(2,1)S(1)}, u32[]{:S(2)}, u32[]{:S(2)}) %all-to-all-start.2) | async-done | bytes 802848 | tf_op jit(solution)/shard_map/all_to_all | solution.py:36
  231.3 1.4 gather_fusion.1
  232.9 1.2 reduce.6
  234.1 1.2 reshape.153
  235.4 8.4 %all-to-all-start.3 = ((bf16[128,2,1568]{2,1,0:T(2,128)(2,1)}), bf16[128,2,1568]{2,1,0:T(2,128)(2,1)S(1)}, u32[]{:S(2)}, u32[]{:S(2)}) async-start(bf16[128,2,1568]{2,1,0:T(2,128)(2,1)} %reshape.153), calls=%async_computation.4 | async-start | bytes 1703936 | tf_op jit(solution)/shard_map/all_to_all | solution.py:38
  244.3 23.3 %all-to-all-done.3 = bf16[128,2,1568]{2,1,0:T(2,128)(2,1)S(1)} async-done(((bf16[128,2,1568]{2,1,0:T(2,128)(2,1)}), bf16[128,2,1568]{2,1,0:T(2,128)(2,1)S(1)}, u32[]{:S(2)}, u32[]{:S(2)}) %all-to-all-start.3) | async-done | bytes 802848 | tf_op jit(solution)/shard_map/all_to_all | solution.py:38
  268.4 1.8 convert_bitcast_fusion
  270.2 1.6 reshape.119
  271.8 2.7 convert_reduce_fusion
  274.6 7.9 %all-reduce = (f32[2,128]{1,0:T(2,128)S(1)}, f32[2]{0:T(128)S(1)}) all-reduce(f32[2,128]{1,0:T(2,128)S(1)} %fusion.21, f32[2]{0:T(128)S(1)} %fusion.9), channel_id=1, replica_groups=mesh['dp'=128,'mp'=4] {'mp'}, use_global_device_ids=true, to_apply=%region_9.11 | all-reduce | flops 258 | bytes 2064 | tf_op jit(solution)/shard_map/psum | solution.py:103
  282.8 155.4 %all-gather = bf16[128,2,128]{2,1,0:T(2,128)(2,1)S(1)} all-gather(bf16[1,2,128]{2,1,0:T(2,128)(2,1)S(1)} %bitcast.69), channel_id=1, replica_groups=mesh['dp'=128,'mp'=4] {'dp'}, dimensions={0}, use_global_device_ids=true | all-gather | bytes 66048 | tf_op jit(solution)/shard_map/all_gather | solution.py:121
  (79 shorter events, 13.8 us)
Async XLA Ops:
  7.2 236.8 %copy-start = (bf16[1024,128]{1,0:T(8,128)(2,1)S(1)}, bf16[1024,128]{1,0:T(8,128)(2,1)}, u32[]{:S(2)}) copy-start(bf16[1024,128]{1,0:T(8,128)(2,1)} %param.31) | copy-start | bytes 786436
  9.0 18.5 %copy-start.6 = (s32[256]{0:T(256)S(1)}, s32[256]{0:T(256)}, u32[]{:S(2)}) copy-start(s32[256]{0:T(256)} %param.18) | copy-start | bytes 3076
  10.8 40.4 %all-to-all-start = ((bf16[2,128,1568]{2,0,1:T(2,128)(2,1)}), bf16[2,128,1568]{2,0,1:T(2,128)(2,1)S(1)}, u32[]{:S(2)}, u32[]{:S(2)}) async-start(bf16[2,128,1568]{2,0,1:T(2,128)(2,1)} %copy.32), calls=%async_computation | async-start | bytes 1703936 | tf_op jit(solution)/shard_map/all_to_all | solution.py:24
  27.4 98.5 %reduce-scatter.2.cloned.1.call-start = ((), (), s32[]{:S(2)}) async-start(), calls=%async_computation.5 | async-start | bytes 1024000 | tf_op jit(solution)/shard_map/reduce_scatter | solution.py:69
  94.5 0.7 copy-start.2
  95.3 32.9 %copy-start.9 = (f32[16]{0:T(128)S(1)}, f32[16]{0:T(128)}, u32[]{:S(2)}) copy-start(f32[16]{0:T(128)} %param.22) | copy-start | bytes 196
  95.3 32.9 %copy-start.10 = (f32[16]{0:T(128)S(1)}, f32[16]{0:T(128)}, u32[]{:S(2)}) copy-start(f32[16]{0:T(128)} %param.21) | copy-start | bytes 196
  153.3 1.2 copy-start.5
  153.3 1.2 copy-start.15
  167.2 0.7 copy-start.11
  167.2 0.7 copy-start.12
  167.6 14.2 %copy-start.3 = (bf16[64,64]{1,0:T(8,128)(2,1)S(1)}, bf16[64,64]{1,0:T(8,128)(2,1)}, u32[]{:S(2)}) copy-start(bf16[64,64]{1,0:T(8,128)(2,1)} %param.26) | copy-start | bytes 24580
  181.7 0.8 copy-start.13
  181.7 0.8 copy-start.14
  183.4 23.5 %copy-start.7 = (s32[256]{0:T(256)S(1)}, s32[256]{0:T(256)}, u32[]{:S(2)}) copy-start(s32[256]{0:T(256)} %param.19) | copy-start | bytes 3076
  185.2 45.4 %all-to-all-start.2 = ((bf16[2,128,1568]{2,0,1:T(2,128)(2,1)}), bf16[2,128,1568]{2,0,1:T(2,128)(2,1)S(1)}, u32[]{:S(2)}, u32[]{:S(2)}) async-start(bf16[2,128,1568]{2,0,1:T(2,128)(2,1)} %copy.39), calls=%async_computation.3 | async-start | bytes 1703936 | tf_op jit(solution)/shard_map/all_to_all | solution.py:36
  234.1 9.7 %copy-start.8 = (f32[2,128]{1,0:T(2,128)S(1)}, f32[2,128]{1,0:T(2,128)}, u32[]{:S(2)}) copy-start(f32[2,128]{1,0:T(2,128)} %param.30) | copy-start | bytes 3076
  235.4 32.2 %all-to-all-start.3 = ((bf16[128,2,1568]{2,1,0:T(2,128)(2,1)}), bf16[128,2,1568]{2,1,0:T(2,128)(2,1)S(1)}, u32[]{:S(2)}, u32[]{:S(2)}) async-start(bf16[128,2,1568]{2,1,0:T(2,128)(2,1)} %reshape.153), calls=%async_computation.4 | async-start | bytes 1703936 | tf_op jit(solution)/shard_map/all_to_all | solution.py:38
  270.2 1.6 copy-start.1
  271.8 2.7 copy-start.4
Sparse Core Ops, SparseCore 0:
  96.7 29.2 reduce-scatter.1
where the time goes:
time: 453 us; the launch traced here: 447 us
  blocking collectives  226 us (50%)
  waiting for transfers between devices  100 us (22%)
  starting transfers between devices  46.8 us (10%)
  local copies, waits for them, and re-layouts  27.4 us (6%)
  other arithmetic  22.1 us (5%)
  between operations  14.7 us (3%)
  matrix products  9.23 us (2%)
    all_gather x1, blocking collectives, on_device(): lax.all_gather(momentum_embeddings_out, 'dp', axis=0, tiled=True)  155 us
    all_to_all x1, blocking collectives, reshuffle_pictures(): lax.all_to_all(columns.reshape(batch * groups, 1, -1), 'dp', split_axis=0...  32.5 us
    reduce_scatter x1, waiting for transfers between devices, on_device(): lax.psum_scatter(partial_sums.astype(jnp.bfloat16), 'mp', scatter_dimensi...  29.4 us
    all_to_all x1, waiting for transfers between devices, restore_images(): lax.all_to_all(tensor_arrangement, 'dp', split_axis=1, concat_axis=0, til...  23.7 us
    all_to_all x1, waiting for transfers between devices, reshuffle_pictures(): lax.all_to_all(tensor_arrangement, 'dp', split_axis=1, concat_axis=0, til...  23.6 us
    all_to_all x1, waiting for transfers between devices, restore_images(): lax.all_to_all(columns.reshape(batch * groups, 1, -1), 'dp', split_axis=0...  23.3 us
    all_to_all x1, starting transfers between devices, restore_images(): lax.all_to_all(tensor_arrangement, 'dp', split_axis=1, concat_axis=0, til...  21.6 us
    all_gather x1, blocking collectives, on_device(): portion = lax.all_gather(first, 'mp', axis=1, tiled=True)  17 us
  transfers between devices with their start and end apart: 4, of which 4 were waited for; matrix products, arithmetic and copies ran while one was open for 0% of the time, Pallas kernels for 0%

commit v1 on v0

v1 whole, which is shorter than its diff:
```python
import jax
import jax.numpy as jnp
from jax import lax
from jax.experimental import pallas as pl
from jax.experimental.pallas import tpu as pltpu
from jax.sharding import PartitionSpec as P

MESH = pl.DeviceIdType.MESH
F32 = jnp.float32
BF16 = jnp.bfloat16

SIDE = 56
PIXELS = SIDE * SIDE
COLS = 64
CHIPS = 64
ROWS = 16
QUARTER = PIXELS // 4 // 16
FULL = ROWS * SIDE // 16
HALF = FULL // 2
BACK = QUARTER + 1
A_TILES = 25
COUNT = 2.0 * (PIXELS // 4)
DIVISOR = 0.2


def nt(a, b):
    return lax.dot_general(a, b, (((1,), (1,)), ((), ())), preferred_element_type=F32)


def tn(a, b):
    return lax.dot_general(a, b, (((0,), (1,)), ((), ())), preferred_element_type=F32)


def remote(src, dst, send, recv, device):
    return pltpu.make_async_remote_copy(
        src_ref=src,
        dst_ref=dst,
        send_sem=send,
        recv_sem=recv,
        device_id=device,
        device_id_type=MESH,
    )


def bytes_of(ref, sem):
    pltpu.make_async_copy(ref, ref, sem).wait()


def kernel(
    perm,
    inv,
    img_hbm,
    rw,
    cw,
    we,
    vin,
    proj,
    queries,
    bank,
    feat,
    score_out,
    loss_out,
    img,
    part,
    from_left,
    from_right,
    via_left,
    via_right,
    sum_a,
    sum_b,
    conv_w,
    exp_w,
    vecs,
    field,
    hold1,
    out1,
    group,
    stat1,
    stat2,
    stat3s,
    stat3,
    mid,
    hold2,
    out2,
    home,
    second_all,
    emb,
    keys1,
    keys2,
    img_sem,
    rs_send,
    rs_recv,
    w_send,
    w_recv,
    s_send,
    s_recv,
    hop_send,
    hop_recv,
    pair_send,
    pair_recv,
    ag_send,
    ag_recv,
    e_send,
    e_recv,
    k_send,
    k_recv,
):
    dp = lax.axis_index("dp")
    mp = lax.axis_index("mp")
    me = dp // 2
    core = dp % 2
    other = dp + 1 - 2 * core
    right = (mp + 1) % 4
    left = (mp + 3) % 4
    far = (mp + 2) % 4

    fetch = pltpu.make_async_copy(img_hbm, img, img_sem)
    fetch.start()

    barrier = pltpu.get_barrier_semaphore()

    def greet(i, carry):
        for u in range(7):
            h = (me + 1 + 7 * i + u) % CHIPS
            pl.semaphore_signal(barrier, inc=1, device_id=(h * 2 + core, mp), device_id_type=MESH)
        return carry

    for j in range(1, 4):
        pl.semaphore_signal(barrier, inc=1, device_id=(dp, (mp + j) % 4), device_id_type=MESH)
    for j in range(4):
        pl.semaphore_signal(barrier, inc=1, device_id=(other, (mp + j) % 4), device_id_type=MESH)
    lax.fori_loop(0, 9, greet, 0)

    row128 = lax.broadcasted_iota(jnp.int32, (128, 384), 0) // 64
    lane128 = (lax.broadcasted_iota(jnp.int32, (128, 384), 1) // 64) % 2
    same = row128 == lane128
    eye_block = same[:, 0:128]

    def doubled(w):
        w = w.astype(F32)
        return jnp.concatenate([w, w], axis=1)

    def diagonal(w):
        return jnp.where(eye_block, jnp.concatenate([w, w], axis=0), 0.0).astype(BF16)

    rw_block = diagonal(doubled(rw[...]))
    we_wide = doubled(we[...])
    we_block = diagonal(we_wide)
    v_row = lax.broadcasted_iota(jnp.int32, (8, 192), 0)
    v_lane = lax.broadcasted_iota(jnp.int32, (8, 192), 1)
    v_in = jnp.where(v_lane // 16 == v_row, jnp.broadcast_to(vin[...], (8, 192)), 0.0)
    v_in = jnp.where(v_row < 4, v_in, 0.0)
    p_row = lax.broadcasted_iota(jnp.int32, (192, 128), 0)
    p_lane = lax.broadcasted_iota(jnp.int32, (192, 128), 1)
    v_place = jnp.where(p_row % 16 + 16 * mp == p_lane % 64, 1.0, 0.0)
    vec = jnp.dot(v_in, v_place, precision=lax.Precision.HIGHEST, preferred_element_type=F32)
    c_row = lax.broadcasted_iota(jnp.int32, (128, 192), 0) % 64
    c_lane = lax.broadcasted_iota(jnp.int32, (128, 192), 1)
    v_all = jnp.broadcast_to(vin[...], (128, 192))
    gain_c = jnp.sum(jnp.where(c_lane == c_row + 64, v_all, 0.0), axis=1, keepdims=True)
    shift_c = jnp.sum(jnp.where(c_lane == c_row + 128, v_all, 0.0), axis=1, keepdims=True)
    fetch.wait()

    part[0:3] = jnp.zeros((3, 16, 128), BF16)
    tail = jnp.zeros((8, 128), F32)
    for k in range(5):
        wide = 640 if k < 4 else 576
        block = tn(img[:, 640 * k : 640 * k + wide], rw_block)
        if k < 4:
            rows = jnp.concatenate([tail, block[:632]], axis=0)
            tail = block[632:640]
        else:
            rows = jnp.concatenate([tail, block, jnp.zeros((56, 128), F32)], axis=0)
        part[40 * k + 3 : 40 * k + 43] = rows.astype(BF16).reshape(40, 16, 128)

    conv_w[mp] = cw[...]
    exp_w[mp] = we_wide.astype(BF16)
    vecs[mp] = vec

    pl.semaphore_wait(barrier, CHIPS - 1 + 7)

    def tiles(q, start, n):
        return part.at[pl.ds(QUARTER * q + start, n)]

    to_r = (dp, right)
    to_l = (dp, left)
    rs = [
        remote(tiles(far, 0, HALF), via_left, rs_send.at[0], rs_recv.at[0], to_r),
        remote(tiles(far, HALF, HALF), via_right, rs_send.at[1], rs_recv.at[1], to_l),
        remote(tiles(right, HALF, HALF), from_left.at[pl.ds(HALF, HALF)], rs_send.at[2], rs_recv.at[2], to_r),
        remote(tiles(left, 0, HALF), from_right.at[pl.ds(0, HALF)], rs_send.at[3], rs_recv.at[3], to_l),
        remote(sum_a, from_left.at[pl.ds(0, HALF)], rs_send.at[4], rs_recv.at[4], to_r),
        remote(sum_b, from_right.at[pl.ds(HALF, HALF)], rs_send.at[5], rs_recv.at[5], to_l),
    ]
    for copy in rs[:4]:
        copy.start()

    def share(buf, n):
        copies = [
            remote(buf.at[mp], buf.at[mp], w_send.at[n, j - 1], w_recv.at[n, j - 1], (dp, (mp + j) % 4))
            for j in range(1, 4)
        ]
        for copy in copies:
            copy.start()
        return copies

    def shared(buf, copies, n):
        for j in range(1, 4):
            src = buf.at[(mp + 4 - j) % 4]
            bytes_of(src, w_recv.at[n, j - 1])

    sent = []

    q_row = lax.broadcasted_iota(jnp.int32, (16, 128), 0)
    q_all = jnp.where(q_row == 0, queries[0:1, :], jnp.where(q_row == 1, queries[1:2, :], 0.0))
    unit = (q_all * lax.rsqrt(jnp.sum(q_all * q_all, axis=1, keepdims=True) + 1e-06)).astype(BF16)
    stored = nt(unit, bank[...]) / DIVISOR
    mass = jnp.broadcast_to(jnp.sum(jnp.exp(stored), axis=1, keepdims=True), (16, 128))

    rs[0].wait_recv()
    own = part[pl.ds(QUARTER * right, HALF)].astype(F32)
    sum_a[...] = (own + via_left[...].astype(F32)).astype(BF16)
    rs[4].start()
    rs[1].wait_recv()
    own = part[pl.ds(QUARTER * left + HALF, HALF)].astype(F32)
    sum_b[...] = (own + via_right[...].astype(F32)).astype(BF16)
    rs[5].start()

    sent += share(conv_w, 0)
    sent += share(exp_w, 1)
    sent += share(vecs, 2)

    for copy in rs[2:]:
        copy.wait_recv()
    total = (
        part[pl.ds(QUARTER * mp, FULL)].astype(F32)
        + from_left[...].astype(F32)
        + from_right[...].astype(F32)
    )
    total = total.reshape(ROWS, SIDE, 128)
    total = jnp.concatenate([total, jnp.zeros((ROWS, COLS - SIDE, 128), F32)], axis=1)
    field[...] = total.reshape(CHIPS, 16, 128).astype(BF16)

    low = lax.broadcasted_iota(jnp.int32, (16, 128), 1) < 64

    def send_tile(src, hold, h, slot):
        remote(
            src.at[h], hold.at[me, core, 0], hop_send.at[slot], hop_recv.at[slot], (h * 2 + core, mp)
        ).start()

    def spread(src, hold, late, n, slot):
        def step(i, carry):
            for u in range(7):
                h = (me + 1 + 7 * i + u) % CHIPS

                @pl.when(jnp.logical_and(h != late, h < n))
                def _():
                    send_tile(src, hold, h, slot)

            return carry

        lax.fori_loop(0, 9, step, 0)

        @pl.when(jnp.logical_and(me != late, me < n))
        def _():
            hold[me, core, 0] = src[me]

    def spread_late(src, hold, late, slot):
        @pl.when(me != late)
        def _():
            send_tile(src, hold, late, slot)

        @pl.when(me == late)
        def _():
            hold[late, core, 0] = src[late]

    def permute(hold, order, out, dst, n, slot):
        def turn(side):
            x = hold[:, side, 0].reshape(CHIPS * 16, 128).astype(F32)
            hold[:, side, 1] = pltpu.roll(x, 64, 1).astype(BF16).reshape(CHIPS, 16, 128)

        def pick(t):
            at = 4 * t + 2 * core
            i0 = order[at]
            i1 = order[at + 1]
            x0 = hold[i0 >> 2, (i0 >> 1) & 1, i0 & 1]
            x1 = hold[i1 >> 2, (i1 >> 1) & 1, 1 - (i1 & 1)]
            return jnp.where(low, x0, x1)

        @pl.when(me < n)
        def _():
            bytes_of(hold.at[pl.ds(0, CHIPS - 1), core, 0], hop_recv.at[slot])
            swap = remote(
                hold.at[:, core, 0], hold.at[:, core, 0], pair_send.at[slot], pair_recv.at[slot], (other, mp)
            )
            swap.start()
            turn(core)
            bytes_of(hold.at[:, 1 - core, 0], pair_recv.at[slot])
            turn(1 - core)

            def step(i, carry):
                ts = [(me + 1 + 9 * i + u) % CHIPS for u in range(9)]
                values = [pick(t) for t in ts]
                for t, value in zip(ts, values):
                    out[t] = value
                for t in ts:
                    remote(
                        out.at[t],
                        dst.at[me],
                        hop_send.at[slot + 1],
                        hop_recv.at[slot + 1],
                        (t * 2 + core, mp),
                    ).start()
                return carry

            lax.fori_loop(0, 7, step, 0)
            dst[me] = pick(me)
            swap.wait_send()
            bytes_of(dst.at[pl.ds(0, n - 1)], hop_recv.at[slot + 1])

        if n < CHIPS:

            @pl.when(me >= n)
            def _():
                bytes_of(dst, hop_recv.at[slot + 1])

    def both(x):
        x = jnp.broadcast_to(x, (8, 128))
        return x + pltpu.roll(x, 64, 1)

    def offer(buf, tile, n):
        buf[mp] = tile
        copies = [
            remote(buf.at[mp], buf.at[mp], s_send.at[n, j - 1], s_recv.at[n, j - 1], (dp, (mp + j) % 4))
            for j in range(1, 4)
        ]
        for copy in copies:
            copy.start()
        return copies

    def collect(buf, n):
        for j in range(1, 4):
            bytes_of(buf.at[(mp + 4 - j) % 4], s_recv.at[n, j - 1])

    def local_stats(x):
        mean = both(jnp.sum(x, axis=0, keepdims=True)) / COUNT
        dev = x - mean[0:1]
        square = both(jnp.sum(dev * dev, axis=0, keepdims=True))
        return jnp.concatenate([mean, square], axis=0)

    def whole_stats(buf, count):
        means = [buf[q, 0:1, :] for q in range(4)]
        mean = (means[0] + means[1] + means[2] + means[3]) * 0.25
        square = jnp.zeros((1, 128), F32)
        for q in range(4):
            off = means[q] - mean
            square = square + buf[q, 8:9, :] + count * (off * off)
        return mean, square / (4.0 * count)

    def pieces(v):
        a = v.astype(BF16).astype(F32)
        b = (v - a).astype(BF16).astype(F32)
        return [a, b, v - a - b]

    spread(field, hold1, 3, CHIPS, 0)
    x = field[...].reshape(ROWS * COLS, 128).astype(F32)
    at = lax.broadcasted_iota(jnp.int32, (ROWS * COLS, 128), 0)
    line = at // COLS
    column = at % COLS
    inner = jnp.logical_and(jnp.logical_and(line >= 1, line <= ROWS - 2), column < SIDE)
    half_count = COUNT / 2.0
    mean = jnp.sum(jnp.where(inner, x, 0.0), axis=0, keepdims=True) / half_count
    dev = jnp.where(inner, x - mean, 0.0)
    square = jnp.sum(dev * dev, axis=0, keepdims=True)
    tile = jnp.concatenate([jnp.broadcast_to(mean, (8, 128)), jnp.broadcast_to(square, (8, 128))], axis=0)
    sent_stats = offer(stat1, tile, 0)
    collect(stat1, 0)
    mean, var = whole_stats(stat1, half_count)
    tile = field[3].astype(F32)
    for r, v in enumerate(pieces(mean) + pieces(var)):
        tile = jnp.where(q_row == 8 + r, v, tile)
    field[3] = tile.astype(BF16)
    spread_late(field, hold1, 3, 0)

    for n, buf in enumerate((conv_w, exp_w, vecs)):
        shared(buf, sent, n)
    conv_blocks = []
    for dy in range(3):
        w = jnp.concatenate([conv_w[q, dy] for q in range(4)] * 2, axis=0).astype(F32)
        conv_blocks.append(jnp.where(same, w, 0.0).astype(BF16))
    vec_all = vecs[0] + vecs[1] + vecs[2] + vecs[3]
    permute(hold1, perm, out1, group, CHIPS, 0)


    marks = group[3].astype(F32)
    mean_i = marks[8:9] + marks[9:10] + marks[10:11]
    var_i = marks[11:12] + marks[12:13] + marks[13:14]
    mean = (both(mean_i) * 0.5)[0:1]
    off = mean_i - mean
    var = (both(var_i + off * off) * 0.5)[0:1]
    x = group[...].reshape(ROWS * COLS, 128).astype(F32)
    true_line = line + (ROWS - 2) * mp - 1
    inside = jnp.logical_and(jnp.logical_and(true_line >= 0, true_line < SIDE), column < SIDE)
    first = jnp.maximum((x - mean) * lax.rsqrt(var + 1e-05) * vec_all[0:1] + vec_all[1:2], 0.0)
    first = jnp.where(inside, first, 0.0)

    wide = jnp.concatenate(
        [
            pltpu.roll(first, 1, 0).astype(BF16),
            first.astype(BF16),
            pltpu.roll(first, ROWS * COLS - 1, 0).astype(BF16),
        ],
        axis=1,
    )
    n_out = (ROWS - 2) * COLS
    spatial = nt(wide[0:n_out], conv_blocks[0])
    spatial = spatial + nt(wide[COLS : COLS + n_out], conv_blocks[1])
    spatial = spatial + nt(wide[2 * COLS : 2 * COLS + n_out], conv_blocks[2])
    spatial = spatial.reshape(ROWS - 2, COLS, 128)[:, :SIDE, :].reshape(16 * QUARTER, 128)

    sent_stats += offer(stat2, local_stats(spatial), 1)
    collect(stat2, 1)
    mean, var = whole_stats(stat2, COUNT)
    second = jnp.maximum((spatial - mean) * lax.rsqrt(var + 1e-05) * vec_all[2:3] + vec_all[3:4], 0.0).astype(BF16)
    mid[0:QUARTER] = second.reshape(QUARTER, 16, 128)
    spread(mid, hold2, QUARTER, QUARTER, 2)

    copies3 = []
    for q in range(4):
        stat3s[q] = local_stats(nt(second, diagonal(exp_w[q].astype(F32))))
    for j in range(1, 4):
        q = (mp + j) % 4
        copy = remote(stat3s.at[q], stat3.at[mp], s_send.at[2, j - 1], s_recv.at[2, j - 1], (dp, q))
        copy.start()
        copies3.append(copy)
    stat3[mp] = stat3s[mp]
    collect(stat3, 2)
    sent_stats += copies3
    mean, var = whole_stats(stat3, COUNT)
    scale = lax.rsqrt(var + 1e-05)
    tile = jnp.zeros((16, 128), F32)
    for r, v in enumerate(pieces(mean) + pieces(scale)):
        tile = jnp.where(q_row == r, v, tile)
    mid[QUARTER] = tile.astype(BF16)
    spread_late(mid, hold2, QUARTER, 2)
    permute(hold2, inv, out2, home, BACK, 2)

    second_all[pl.ds(QUARTER * mp, QUARTER)] = home[0:QUARTER]
    b_tiles = QUARTER - A_TILES

    def a_of(q):
        return second_all.at[pl.ds(QUARTER * q, A_TILES)]

    def b_of(q):
        return second_all.at[pl.ds(QUARTER * q + A_TILES, b_tiles)]

    ag = [
        remote(a_of(mp), a_of(mp), ag_send.at[0], ag_recv.at[0], to_r),
        remote(b_of(mp), b_of(mp), ag_send.at[1], ag_recv.at[1], to_l),
        remote(b_of(mp), b_of(mp), ag_send.at[2], ag_recv.at[2], to_r),
        remote(a_of(mp), a_of(mp), ag_send.at[3], ag_recv.at[3], to_l),
        remote(a_of(left), a_of(left), ag_send.at[4], ag_recv.at[4], to_r),
        remote(b_of(right), b_of(right), ag_send.at[5], ag_recv.at[5], to_l),
    ]
    for copy in ag[:4]:
        copy.start()
    bytes_of(a_of(left), ag_recv.at[0])
    ag[4].start()
    bytes_of(b_of(right), ag_recv.at[1])
    ag[5].start()

    identity = jnp.where(
        lax.broadcasted_iota(jnp.int32, (128, 128), 0) == lax.broadcasted_iota(jnp.int32, (128, 128), 1),
        1.0,
        0.0,
    ).astype(BF16)
    columns = nt(identity, home[QUARTER])
    mean_c = columns[:, 0:1] + columns[:, 1:2] + columns[:, 2:3]
    scale_c = columns[:, 3:4] + columns[:, 4:5] + columns[:, 5:6]

    bytes_of(b_of(left), ag_recv.at[2])
    bytes_of(a_of(right), ag_recv.at[3])
    bytes_of(a_of(far), ag_recv.at[4])
    bytes_of(b_of(far), ag_recv.at[5])

    pooled = jnp.zeros((128, 1), F32)
    for k in range(5):
        n = 40 if k < 4 else 36
        block = second_all[40 * k : 40 * k + n].reshape(16 * n, 128)
        v = nt(we_block, block)
        third = ((v - mean_c) * scale_c * gain_c + shift_c).astype(BF16).astype(F32)
        lanes = slice(640 * k, 640 * k + 16 * n)
        f = jnp.maximum(third + img[:, lanes].astype(F32), 0.0).astype(BF16)
        feat[:, lanes] = f
        pooled = pooled + jnp.sum(f.astype(F32), axis=1, keepdims=True)
    pooled = pooled / float(PIXELS)

    proj2 = jnp.concatenate([proj[...], proj[...]], axis=0).astype(F32)
    terms = pooled * proj2
    e0 = jnp.sum(terms[0:64], axis=0, keepdims=True)
    e1 = jnp.sum(terms[64:128], axis=0, keepdims=True)
    row8 = lax.broadcasted_iota(jnp.int32, (8, 128), 0)
    top = jnp.where(row8 == 0, e0, jnp.where(row8 == 1, e1, 0.0))
    emb[core, mp] = jnp.concatenate([top, mass[0:8]], axis=0)
    mine = emb.at[core, mp]
    e_copies = []
    for j in range(1, 4):
        e_copies.append(remote(mine, mine, e_send.at[j], e_recv.at[j], (dp, (mp + j) % 4)))
    for j in range(4):
        e_copies.append(remote(mine, mine, e_send.at[4 + j], e_recv.at[4 + j], (other, (mp + j) % 4)))
    for copy in e_copies:
        copy.start()
    for j in range(1, 4):
        bytes_of(emb.at[core, (mp + 4 - j) % 4], e_recv.at[j])
    for j in range(4):
        bytes_of(emb.at[1 - core, (mp + 4 - j) % 4], e_recv.at[4 + j])

    key_tile = jnp.zeros((16, 128), F32)
    for cc in range(2):
        e = emb[cc, 0, 0:8] + emb[cc, 1, 0:8] + emb[cc, 2, 0:8] + emb[cc, 3, 0:8]
        key = e * lax.rsqrt(jnp.sum(e * e, axis=1, keepdims=True) + 1e-06)
        for b in range(2):
            here = q_row == 4 * (me % 4) + 2 * cc + b
            key_tile = jnp.where(here, key[b : b + 1], key_tile)
    queue = emb[core, 0, 8:16] + emb[core, 1, 8:16] + emb[core, 2, 8:16] + emb[core, 3, 8:16]
    z = me % 8
    slab = me // 8
    keys1[z] = key_tile.astype(BF16)
    k_copies = []
    for j in range(1, 8):
        h = slab * 8 + (z + j) % 8
        k_copies.append(remote(keys1.at[z], keys1.at[z], k_send.at[0, j], k_recv.at[0, j], (h * 2 + core, mp)))
    for copy in k_copies:
        copy.start()
    for j in range(1, 8):
        bytes_of(keys1.at[(z + 8 - j) % 8], k_recv.at[0, j])
    keys2[slab] = jnp.sum(keys1[...].astype(F32).reshape(2, 4, 16, 128), axis=1).astype(BF16)
    k_copies2 = []
    for j in range(1, 8):
        h = (me + 8 * j) % CHIPS
        k_copies2.append(
            remote(keys2.at[slab], keys2.at[slab], k_send.at[1, j], k_recv.at[1, j], (h * 2 + core, mp))
        )
    for copy in k_copies2:
        copy.start()
    for j in range(1, 8):
        bytes_of(keys2.at[(slab + 8 - j) % 8], k_recv.at[1, j])
    every = keys2[...].reshape(256, 128)
    score = (nt(unit, every) / DIVISOR)[0:8]
    score_out[...] = score[0:2]
    lane = lax.broadcasted_iota(jnp.int32, (8, 256), 1)
    row = lax.broadcasted_iota(jnp.int32, (8, 256), 0)
    matched = jnp.sum(jnp.where(lane == 2 * dp + row, score, 0.0), axis=1, keepdims=True)
    mass_all = jnp.sum(jnp.exp(score), axis=1, keepdims=True) + queue[:, 0:1]
    losses = jnp.broadcast_to(jnp.log(mass_all) - matched, (8, 128))
    lane8 = lax.broadcasted_iota(jnp.int32, (8, 128), 1)
    loss_out[...] = jnp.sum(jnp.where(row8 == lane8, losses, 0.0), axis=0, keepdims=True)[:, 0:2]

    for copy in rs + sent + sent_stats + ag + e_copies + k_copies + k_copies2:
        copy.wait_send()
    bytes_of(field.at[pl.ds(0, CHIPS - 1)], hop_send.at[0])
    bytes_of(out1.at[pl.ds(0, CHIPS - 1)], hop_send.at[1])

    @pl.when(me < BACK)
    def _():
        bytes_of(mid.at[pl.ds(0, BACK - 1)], hop_send.at[2])
        bytes_of(out2.at[pl.ds(0, CHIPS - 1)], hop_send.at[3])

    @pl.when(me >= BACK)
    def _():
        bytes_of(mid, hop_send.at[2])


def on_device(
    images,
    permutation,
    inverse,
    reduce_weight,
    reduce_gain,
    reduce_shift,
    spatial_weight,
    spatial_gain,
    spatial_shift,
    expand_weight,
    expand_gain,
    expand_shift,
    projection,
    queries,
    dictionary_bank,
):
    cw = jnp.transpose(spatial_weight, (2, 0, 3, 1))
    cw = jnp.stack([cw, cw], axis=3).reshape(3, 16, 384)
    vin = jnp.concatenate(
        [reduce_gain, reduce_shift, spatial_gain, spatial_shift, expand_gain, expand_shift]
    ).reshape(1, 192)

    vmem = pl.BlockSpec(memory_space=pltpu.VMEM)
    smem = pl.BlockSpec(memory_space=pltpu.SMEM)
    dma = pltpu.SemaphoreType.DMA
    feat, score, loss = pl.pallas_call(
        kernel,
        out_shape=(
            jax.ShapeDtypeStruct((128, PIXELS), BF16),
            jax.ShapeDtypeStruct((2, 256), F32),
            jax.ShapeDtypeStruct((1, 2), F32),
        ),
        in_specs=[smem, smem, pl.BlockSpec(memory_space=pl.ANY)] + [vmem] * 7,
        out_specs=(vmem, vmem, vmem),
        scratch_shapes=[
            pltpu.VMEM((128, PIXELS), BF16),
            pltpu.VMEM((203, 16, 128), BF16),
            pltpu.VMEM((FULL, 16, 128), BF16),
            pltpu.VMEM((FULL, 16, 128), BF16),
            pltpu.VMEM((HALF, 16, 128), BF16),
            pltpu.VMEM((HALF, 16, 128), BF16),
            pltpu.VMEM((HALF, 16, 128), BF16),
            pltpu.VMEM((HALF, 16, 128), BF16),
            pltpu.VMEM((4, 3, 16, 384), BF16),
            pltpu.VMEM((4, 64, 128), BF16),
            pltpu.VMEM((4, 8, 128), F32),
            pltpu.VMEM((CHIPS, 16, 128), BF16),
            pltpu.VMEM((CHIPS, 2, 2, 16, 128), BF16),
            pltpu.VMEM((CHIPS, 16, 128), BF16),
            pltpu.VMEM((CHIPS, 16, 128), BF16),
            pltpu.VMEM((4, 16, 128), F32),
            pltpu.VMEM((4, 16, 128), F32),
            pltpu.VMEM((4, 16, 128), F32),
            pltpu.VMEM((4, 16, 128), F32),
            pltpu.VMEM((BACK, 16, 128), BF16),
            pltpu.VMEM((CHIPS, 2, 2, 16, 128), BF16),
            pltpu.VMEM((CHIPS, 16, 128), BF16),
            pltpu.VMEM((BACK, 16, 128), BF16),
            pltpu.VMEM((4 * QUARTER, 16, 128), BF16),
            pltpu.VMEM((2, 4, 16, 128), F32),
            pltpu.VMEM((8, 16, 128), BF16),
            pltpu.VMEM((8, 2, 16, 128), BF16),
            dma,
            dma((6,)),
            dma((6,)),
            dma((3, 3)),
            dma((3, 3)),
            dma((3, 3)),
            dma((3, 3)),
            dma((4,)),
            dma((4,)),
            dma((4,)),
            dma((4,)),
            dma((6,)),
            dma((6,)),
            dma((8,)),
            dma((8,)),
            dma((2, 8)),
            dma((2, 8)),
        ],
        compiler_params=pltpu.CompilerParams(
            collective_id=0, has_side_effects=True, vmem_limit_bytes=48 * 1024 * 1024
        ),
        cost_estimate=pl.CostEstimate(
            flops=2 * 3136 * 128 * 128 * 4, bytes_accessed=2 * 128 * 3136 * 2, transcendentals=0
        ),
    )(
        permutation,
        inverse,
        images.reshape(128, PIXELS),
        reduce_weight,
        cw,
        expand_weight,
        vin,
        projection,
        queries,
        dictionary_bank,
    )
    return feat.reshape(images.shape), score, loss.reshape(2)


def solution(mesh):
    placed = (
        P("dp", "mp", None),
        P(),
        P(),
        P(None, "mp"),
        P("mp"),
        P("mp"),
        P("mp", None, None, None),
        P("mp"),
        P("mp"),
        P("mp", None),
        P("mp"),
        P("mp"),
        P("mp", None),
        P("dp", None),
        P("mp", None),
    )
    return jax.shard_map(
        on_device,
        mesh=mesh,
        in_specs=placed,
        out_specs=(P("dp", "mp", None), P("dp", None), P("dp")),
        check_vma=False,
    )
```

time: 453 us -> 120 us (0.26); the launches traced: 447 us -> 120 us
  blocking collectives: 226 us -> 0 us
  Pallas kernels: 0 us -> 114 us
  waiting for transfers between devices: 100 us -> 0 us
  starting transfers between devices: 46.8 us -> 0 us
  local copies, waits for them, and re-layouts: 27.4 us -> 4.74 us
  other arithmetic: 22.1 us -> 0.86 us
  between operations: 14.7 us -> 0.72 us
  matrix products: 9.23 us -> 0 us
    all_gather x3 -> x0, blocking collectives: 186 us -> none  [the longest x1 155 us: on_device(): lax.all_gather(momentum_embeddings_out, 'dp', axis=0, tiled=True)]
    pallas_call x0 -> x1, Pallas kernels: none -> 114 us  [on_device(): pl.pallas_call(kernel, out_shape=(jax.ShapeDtypeStruct((128, PIXELS), BF1...]
    all_to_all x3 -> x0, waiting for transfers between devices: 70.6 us -> none  [the longest x1 23.7 us: restore_images(): lax.all_to_all(tensor_arrangement, 'dp', split_axis=1, concat_axis=0, til...]
    all_to_all x3 -> x0, starting transfers between devices: 46.7 us -> none  [the longest x1 21.6 us: restore_images(): lax.all_to_all(tensor_arrangement, 'dp', split_axis=1, concat_axis=0, til...]
    all_to_all x1 -> x0, blocking collectives: 32.5 us -> none  [reshuffle_pictures(): lax.all_to_all(columns.reshape(batch * groups, 1, -1), 'dp', split_axis=0...]
    reduce_scatter x1 -> x0, waiting for transfers between devices: 29.4 us -> none  [on_device(): lax.psum_scatter(partial_sums.astype(jnp.bfloat16), 'mp', scatter_dimensi...]
    reshape x10 -> x1, local copies, waits for them, and re-layouts: 10.5 us -> 0.12 us  [on_device(): cw = jnp.stack([cw, cw], axis=3).reshape(3, 16, 384)]
    reduce_sum x8 -> x0, other arithmetic: 8.75 us -> none  [the longest x3 4.58 us: normalize(): spread = jnp.mean((values - center) ** 2, axis=(0, 2), keepdims=True)]
  transfers between devices with their start and end apart: 4 -> 0, of which waited for: 4 -> 0; matrix products, arithmetic and copies ran while one was open for 0% -> 0% of each run, Pallas kernels for 0% -> 0%
where the time goes in v1:
time: 120 us
  Pallas kernels  114 us (95%)
  local copies, waits for them, and re-layouts  4.74 us (4%)
    pallas_call x1, Pallas kernels, on_device(): pl.pallas_call(kernel, out_shape=(jax.ShapeDtypeStruct((128, PIXELS), BF1...  114 us
    unnamed x19, local copies, waits for them, and re-layouts  3.71 us

profile of v1, /device:TPU:1, one launch (start us, length us, event | category | flops | bytes accessed | tf_op | source)
XLA Modules:
  0.0 120.0 jit_solution(2023086135935005047)
XLA Ops:
  0.6 0.0 copy-start.1
  0.6 0.9 concatenate.3
  1.5 0.9 pad_maximum_fusion
  2.4 0.1 copy.18
  2.4 0.0 copy-start.2
  2.4 0.0 copy-start.3
  2.4 0.0 copy-start.4
  2.5 0.0 copy-start.5
  2.5 0.0 copy-start.6
  2.5 0.0 copy-start.7
  2.5 0.1 reshape.22.cw
  2.6 0.0 copy-done.1
  2.6 0.5 copy-done.2
  3.1 0.0 copy-done.3
  3.2 0.0 copy-done.4
  3.2 0.0 copy-done.5
  3.2 0.0 copy-done.6
  3.2 0.0 copy-done.7
  3.2 0.0 copy-start
  3.2 1.1 copy-done
  4.3 113.7 %shard_map.166 = (bf16[128,3136]{1,0:T(8,128)(2,1)S(1)}, f32[2,256]{1,0:T(2,128)S(1)}, f32[1,2]{1,0:T(1,128)S(1)}) custom-call(s32[256]{0:T(256)S(1)} %copy-done.5, s32[256]{0:T(256)S(1)} %copy-done.6, bf16[128,3136]{1,0:T(8,128)(2,1)S(1)} %bitcast.9, bf16[64,64]{1,0:T(8,128)(2,1)S(1)} %copy-done.2, bf16[3,16,384]{2,1,0:T(8,128)(2,1)S(1)} %reshape.22.cw, ...), custom_call_target="tpu_custom_call" | custom-call | flops 411041792 | bytes 1605632 | tf_op jit(solution)/shard_map/pallas_call | solution.py:600
  118.1 0.9 copy.22
  119.0 0.6 copy.23
  119.5 0.5 copy.24
Async XLA Ops:
  0.6 2.0 %copy-start.1 = (bf16[1024,128]{1,0:T(8,128)(2,1)S(1)}, bf16[1024,128]{1,0:T(8,128)(2,1)}, u32[]{:S(2)}) copy-start(bf16[1024,128]{1,0:T(8,128)(2,1)} %bank.1) | copy-start | bytes 786436
  2.4 0.7 copy-start.2
  2.4 0.7 copy-start.3
  2.4 0.7 copy-start.4
  2.5 0.7 copy-start.5
  2.5 0.7 copy-start.6
  2.5 0.7 copy-start.7
  3.2 1.1 copy-start

commit v2 on v1

v2 whole, which is shorter than its diff:
```python
import jax
import jax.numpy as jnp
from jax import lax
from jax.experimental import pallas as pl
from jax.experimental.pallas import tpu as pltpu
from jax.sharding import PartitionSpec as P

MESH = pl.DeviceIdType.MESH
F32 = jnp.float32
BF16 = jnp.bfloat16

SIDE = 56
PIXELS = SIDE * SIDE
COLS = 64
CHIPS = 64
LINES = SIDE // 4
QUARTER = PIXELS // 4 // 16
A_TILES = 25
B_TILES = QUARTER - A_TILES
BACK = QUARTER + 1
STAT_CHIP = CHIPS - 1
COUNT = 2.0 * (PIXELS // 4)
DIVISOR = 0.2


def nt(a, b):
    return lax.dot_general(a, b, (((1,), (1,)), ((), ())), preferred_element_type=F32)


def tn(a, b):
    return lax.dot_general(a, b, (((0,), (1,)), ((), ())), preferred_element_type=F32)


def remote(src, dst, send, recv, device):
    return pltpu.make_async_remote_copy(
        src_ref=src,
        dst_ref=dst,
        send_sem=send,
        recv_sem=recv,
        device_id=device,
        device_id_type=MESH,
    )


def bytes_of(ref, sem):
    pltpu.make_async_copy(ref, ref, sem).wait()


def kernel(
    perm,
    inv,
    img_hbm,
    rw,
    cw,
    we,
    rg,
    rsh,
    sg,
    ssh,
    eg,
    esh,
    proj,
    queries,
    bank,
    feat_hbm,
    score_out,
    loss_out,
    img,
    feat,
    part,
    from_left,
    from_right,
    via_left,
    via_right,
    sum_a,
    sum_b,
    conv_w,
    exp_w,
    vecs,
    field,
    hold1,
    out1,
    group,
    stat1,
    stat2,
    stat3s,
    stat3,
    mid,
    hold2,
    out2,
    home,
    second_all,
    emb,
    keys1,
    keys2,
    halo_top,
    halo_bottom,
    img_sem,
    feat_sem,
    rs_send,
    rs_recv,
    w_send,
    w_recv,
    s_send,
    s_recv,
    hop_send,
    hop_recv,
    out_send,
    out_recv,
    halo_send,
    halo_recv,
    pair_send,
    pair_recv,
    ag_send,
    ag_recv,
    e_send,
    e_recv,
    k_send,
    k_recv,
):
    dp = lax.axis_index("dp")
    mp = lax.axis_index("mp")
    me = dp // 2
    core = dp % 2
    other = dp + 1 - 2 * core
    right = (mp + 1) % 4
    left = (mp + 3) % 4
    far = (mp + 2) % 4

    fetch = pltpu.make_async_copy(img_hbm, img, img_sem)
    fetch.start()

    barrier = pltpu.get_barrier_semaphore()

    def greet(i, carry):
        for u in range(7):
            h = (me + 1 + 7 * i + u) % CHIPS
            pl.semaphore_signal(barrier, inc=1, device_id=(h * 2 + core, mp), device_id_type=MESH)
        return carry

    for j in range(1, 4):
        pl.semaphore_signal(barrier, inc=1, device_id=(dp, (mp + j) % 4), device_id_type=MESH)
    for j in range(4):
        pl.semaphore_signal(barrier, inc=1, device_id=(other, (mp + j) % 4), device_id_type=MESH)
    lax.fori_loop(0, 9, greet, 0)

    row128 = lax.broadcasted_iota(jnp.int32, (128, 384), 0) // 64
    lane128 = (lax.broadcasted_iota(jnp.int32, (128, 384), 1) // 64) % 2
    same = row128 == lane128
    eye_block = same[:, 0:128]

    def doubled(w):
        w = w.astype(F32)
        return jnp.concatenate([w, w], axis=1)

    def diagonal(w):
        return jnp.where(eye_block, jnp.concatenate([w, w], axis=0), 0.0).astype(BF16)

    rw_block = diagonal(doubled(rw[...]))
    fetch.wait()

    for k in range(5):
        n = 40 if k < 4 else 36
        block = tn(img[:, 640 * k : 640 * k + 16 * n], rw_block)
        part[40 * k : 40 * k + n] = block.astype(BF16).reshape(n, 16, 128)

    pl.semaphore_wait(barrier, CHIPS - 1 + 7)

    def a_part(q):
        return part.at[pl.ds(QUARTER * q, A_TILES)]

    def b_part(q):
        return part.at[pl.ds(QUARTER * q + A_TILES, B_TILES)]

    to_r = (dp, right)
    to_l = (dp, left)
    left_a = from_left.at[pl.ds(0, A_TILES)]
    left_b = from_left.at[pl.ds(A_TILES, B_TILES)]
    right_a = from_right.at[pl.ds(0, A_TILES)]
    right_b = from_right.at[pl.ds(A_TILES, B_TILES)]
    rs = [
        remote(a_part(far), via_left, rs_send.at[0], rs_recv.at[0], to_r),
        remote(a_part(left), right_a, rs_send.at[1], rs_recv.at[1], to_l),
        remote(b_part(right), left_b, rs_send.at[2], rs_recv.at[2], to_r),
        remote(b_part(far), via_right, rs_send.at[3], rs_recv.at[3], to_l),
        remote(sum_a, left_a, rs_send.at[4], rs_recv.at[4], to_r),
        remote(sum_b, right_b, rs_send.at[5], rs_recv.at[5], to_l),
    ]
    for copy in rs[:4]:
        copy.start()

    vin = jnp.concatenate([rg[...], rsh[...], sg[...], ssh[...], eg[...], esh[...]], axis=1)
    we_wide = doubled(we[...])
    we_block = diagonal(we_wide)
    v_row = lax.broadcasted_iota(jnp.int32, (8, 192), 0)
    v_lane = lax.broadcasted_iota(jnp.int32, (8, 192), 1)
    v_in = jnp.where(v_lane // 16 == v_row, jnp.broadcast_to(vin, (8, 192)), 0.0)
    v_in = jnp.where(v_row < 4, v_in, 0.0)
    p_row = lax.broadcasted_iota(jnp.int32, (192, 128), 0)
    p_lane = lax.broadcasted_iota(jnp.int32, (192, 128), 1)
    v_place = jnp.where(p_row % 16 + 16 * mp == p_lane % 64, 1.0, 0.0)
    vec = jnp.dot(v_in, v_place, precision=lax.Precision.HIGHEST, preferred_element_type=F32)
    c_row = lax.broadcasted_iota(jnp.int32, (128, 192), 0) % 64
    c_lane = lax.broadcasted_iota(jnp.int32, (128, 192), 1)
    v_all = jnp.broadcast_to(vin, (128, 192))
    gain_c = jnp.sum(jnp.where(c_lane == c_row + 64, v_all, 0.0), axis=1, keepdims=True)
    shift_c = jnp.sum(jnp.where(c_lane == c_row + 128, v_all, 0.0), axis=1, keepdims=True)
    for dy in range(3):
        conv_w[mp, dy] = jnp.concatenate([doubled(cw[dy, dx]) for dx in range(3)], axis=1).astype(BF16)
    exp_w[mp] = we_wide.astype(BF16)
    vecs[mp] = vec

    def share(buf, n):
        copies = [
            remote(buf.at[mp], buf.at[mp], w_send.at[n, j - 1], w_recv.at[n, j - 1], (dp, (mp + j) % 4))
            for j in range(1, 4)
        ]
        for copy in copies:
            copy.start()
        return copies

    def shared(buf, copies, n):
        for j in range(1, 4):
            src = buf.at[(mp + 4 - j) % 4]
            bytes_of(src, w_recv.at[n, j - 1])

    sent = []

    q_row = lax.broadcasted_iota(jnp.int32, (16, 128), 0)
    q_all = jnp.where(q_row == 0, queries[0:1, :], jnp.where(q_row == 1, queries[1:2, :], 0.0))
    unit = (q_all * lax.rsqrt(jnp.sum(q_all * q_all, axis=1, keepdims=True) + 1e-06)).astype(BF16)
    stored = nt(unit, bank[...]) / DIVISOR
    mass = jnp.broadcast_to(jnp.sum(jnp.exp(stored), axis=1, keepdims=True), (16, 128))

    rs[0].wait_recv()
    own = part[pl.ds(QUARTER * right, A_TILES)].astype(F32)
    sum_a[...] = (own + via_left[...].astype(F32)).astype(BF16)
    rs[4].start()
    rs[3].wait_recv()
    own = part[pl.ds(QUARTER * left + A_TILES, B_TILES)].astype(F32)
    sum_b[...] = (own + via_right[...].astype(F32)).astype(BF16)
    rs[5].start()

    sent += share(conv_w, 0)
    sent += share(exp_w, 1)
    sent += share(vecs, 2)

    low = lax.broadcasted_iota(jnp.int32, (16, 128), 1) < 64
    pair = me // 2
    holds_a = jnp.logical_and(me % 2 == 0, pair < A_TILES)
    holds_b = jnp.logical_and(me % 2 == 1, pair < B_TILES)
    holds_s = me == STAT_CHIP

    def send_tile(src, t, hold, h, slot):
        remote(
            src.at[t],
            hold.at[me, core, 0],
            hop_send.at[slot],
            hop_recv.at[slot, me // 8],
            (h * 2 + core, mp),
        ).start()

    def spread(src, hold, odd, slot):
        n = B_TILES if odd else A_TILES

        def step(i, carry):
            for u in range(8):
                t = (pair + 8 * i + u) % (CHIPS // 2)
                h = 2 * t + odd

                @pl.when(jnp.logical_and(h != me, t < n))
                def _():
                    send_tile(src, t + odd * A_TILES, hold, h, slot)

            return carry

        lax.fori_loop(0, 4, step, 0)

        @pl.when(holds_b if odd else holds_a)
        def _():
            hold[me, core, 0] = src[pair + odd * A_TILES]

    def spread_stats(src, hold, slot):
        @pl.when(me != STAT_CHIP)
        def _():
            send_tile(src, QUARTER, hold, STAT_CHIP, slot)

        @pl.when(holds_s)
        def _():
            hold[STAT_CHIP, core, 0] = src[QUARTER]

    def permute(hold, order, out, dst, slot, holds, tile, part_of):
        def turn(side, g):
            at = pl.ds(8 * g, 8)
            x = hold[at, side, 0].reshape(128, 128).astype(F32)
            hold[at, side, 1] = pltpu.roll(x, 64, 1).astype(BF16).reshape(8, 16, 128)

        def swapping(g):
            ref = hold.at[pl.ds(8 * g, 8), core, 0]
            return remote(ref, ref, pair_send.at[slot, g], pair_recv.at[slot, g], (other, mp))

        def take(i, carry):
            g = (me // 8 + 8 - i) % 8
            bytes_of(hold.at[pl.ds(8 * g, 8), core, 0], hop_recv.at[slot, g])
            swapping(g).start()
            turn(core, g)
            return carry

        def take_other(i, carry):
            g = (me // 8 + 8 - i) % 8
            bytes_of(hold.at[pl.ds(8 * g, 8), 1 - core, 0], pair_recv.at[slot, g])
            turn(1 - core, g)
            return carry

        def swapped(i, carry):
            swapping(i).wait_send()
            return carry

        def pick(t):
            at = 4 * t + 2 * core
            i0 = order[at]
            i1 = order[at + 1]
            x0 = hold[i0 >> 2, (i0 >> 1) & 1, i0 & 1]
            x1 = hold[i1 >> 2, (i1 >> 1) & 1, 1 - (i1 & 1)]
            return jnp.where(low, x0, x1)

        @pl.when(holds)
        def _():
            g = me // 8
            bytes_of(hold.at[pl.ds(8 * g, 7), core, 0], hop_recv.at[slot, g])
            swapping(g).start()
            turn(core, g)
            lax.fori_loop(1, 8, take, 0)
            lax.fori_loop(0, 8, take_other, 0)

            def step(i, carry):
                ts = [(me + 1 + 9 * i + u) % CHIPS for u in range(9)]
                values = [pick(t) for t in ts]
                for t, value in zip(ts, values):
                    out[t] = value
                for t in ts:
                    remote(
                        out.at[t],
                        dst.at[tile],
                        out_send.at[slot],
                        out_recv.at[slot, part_of],
                        (t * 2 + core, mp),
                    ).start()
                return carry

            lax.fori_loop(0, 7, step, 0)
            dst[tile] = pick(me)
            lax.fori_loop(0, 8, swapped, 0)

    def arrived(dst, slot, part_of):
        start, n, holds = ((0, A_TILES, holds_a), (A_TILES, B_TILES, holds_b), (QUARTER, 1, holds_s))[part_of]

        @pl.when(jnp.logical_not(holds))
        def _():
            bytes_of(dst.at[pl.ds(start, n)], out_recv.at[slot, part_of])

        if n > 1:

            @pl.when(holds)
            def _():
                bytes_of(dst.at[pl.ds(start, n - 1)], out_recv.at[slot, part_of])

    rs[4].wait_recv()
    rs[1].wait_recv()
    total = part[pl.ds(QUARTER * mp, A_TILES)].astype(F32)
    total = total + left_a[...].astype(F32) + right_a[...].astype(F32)
    field[0:A_TILES] = total.astype(BF16)
    spread(field, hold1, 0, 0)

    rs[2].wait_recv()
    rs[5].wait_recv()
    total = part[pl.ds(QUARTER * mp + A_TILES, B_TILES)].astype(F32)
    total = total + left_b[...].astype(F32) + right_b[...].astype(F32)
    field[A_TILES:QUARTER] = total.astype(BF16)
    spread(field, hold1, 1, 0)

    def both(x):
        x = jnp.broadcast_to(x, (8, 128))
        return x + pltpu.roll(x, 64, 1)

    def offer(buf, tile, n):
        buf[mp] = tile
        copies = [
            remote(buf.at[mp], buf.at[mp], s_send.at[n, j - 1], s_recv.at[n, j - 1], (dp, (mp + j) % 4))
            for j in range(1, 4)
        ]
        for copy in copies:
            copy.start()
        return copies

    def collect(buf, n):
        for j in range(1, 4):
            bytes_of(buf.at[(mp + 4 - j) % 4], s_recv.at[n, j - 1])

    def local_stats(x):
        mean = both(jnp.sum(x, axis=0, keepdims=True)) / COUNT
        dev = x - mean[0:1]
        square = both(jnp.sum(dev * dev, axis=0, keepdims=True))
        return jnp.concatenate([mean, square], axis=0)

    def whole_stats(buf, count):
        means = [buf[q, 0:1, :] for q in range(4)]
        mean = (means[0] + means[1] + means[2] + means[3]) * 0.25
        square = jnp.zeros((1, 128), F32)
        for q in range(4):
            off = means[q] - mean
            square = square + buf[q, 8:9, :] + count * (off * off)
        return mean, square / (4.0 * count)

    def pieces(v):
        a = v.astype(BF16).astype(F32)
        b = (v - a).astype(BF16).astype(F32)
        return [a, b, v - a - b]

    x = field[0:QUARTER].reshape(16 * QUARTER, 128).astype(F32)
    half_count = COUNT / 2.0
    mean = jnp.sum(x, axis=0, keepdims=True) / half_count
    dev = x - mean
    square = jnp.sum(dev * dev, axis=0, keepdims=True)
    tile = jnp.concatenate([jnp.broadcast_to(mean, (8, 128)), jnp.broadcast_to(square, (8, 128))], axis=0)
    sent_stats = offer(stat1, tile, 0)
    collect(stat1, 0)
    mean, var = whole_stats(stat1, half_count)

    def stat_tile(values):
        tile = jnp.zeros((16, 128), F32)
        for r, v in enumerate(values):
            tile = jnp.where(q_row == r, v, tile)
        return tile.astype(BF16)

    field[QUARTER] = stat_tile(pieces(mean) + pieces(var))
    spread_stats(field, hold1, 0)

    for n, buf in enumerate((conv_w, exp_w, vecs)):
        shared(buf, sent, n)
    conv_blocks = []
    for dy in range(3):
        w = jnp.concatenate([conv_w[q, dy] for q in range(4)] * 2, axis=0).astype(F32)
        conv_blocks.append(jnp.where(same, w, 0.0).astype(BF16))
    vec_all = vecs[0] + vecs[1] + vecs[2] + vecs[3]
    holder = jnp.logical_or(jnp.logical_or(holds_a, holds_b), holds_s)
    held = jnp.where(holds_s, QUARTER, jnp.where(holds_a, pair, pair + A_TILES))
    held_part = jnp.where(holds_s, 2, jnp.where(holds_a, 0, 1))
    permute(hold1, perm, out1, group, 0, holder, held, held_part)
    arrived(group, 0, 0)
    arrived(group, 0, 1)
    halos = [
        remote(group.at[pl.ds(0, 4)], halo_bottom, halo_send.at[0], halo_recv.at[0], to_l),
        remote(group.at[pl.ds(QUARTER - 4, 4)], halo_top, halo_send.at[1], halo_recv.at[1], to_r),
    ]
    for copy in halos:
        copy.start()
    arrived(group, 0, 2)


    marks = group[QUARTER].astype(F32)
    mean_i = marks[0:1] + marks[1:2] + marks[2:3]
    var_i = marks[3:4] + marks[4:5] + marks[5:6]
    mean = (both(mean_i) * 0.5)[0:1]
    off = mean_i - mean
    var = (both(var_i + off * off) * 0.5)[0:1]
    scale = lax.rsqrt(var + 1e-05)

    def norm1(tiles):
        x = tiles.reshape(-1, 128).astype(F32)
        return jnp.maximum((x - mean) * scale * vec_all[0:1] + vec_all[1:2], 0.0)

    inner = norm1(group[0:QUARTER]).reshape(LINES, SIDE, 128)
    for copy in halos:
        copy.wait_recv()
    top = norm1(halo_top[...])[8:64]
    bottom = norm1(halo_bottom[...])[0:SIDE]
    top = jnp.where(jnp.full((SIDE, 128), mp, jnp.int32) == 0, 0.0, top).reshape(1, SIDE, 128)
    bottom = jnp.where(jnp.full((SIDE, 128), mp, jnp.int32) == 3, 0.0, bottom).reshape(1, SIDE, 128)
    first = jnp.concatenate([top, inner, bottom], axis=0)
    first = jnp.concatenate([first, jnp.zeros((LINES + 2, COLS - SIDE, 128), F32)], axis=1)
    first = first.reshape((LINES + 2) * COLS, 128)

    wide = jnp.concatenate(
        [
            pltpu.roll(first, 1, 0).astype(BF16),
            first.astype(BF16),
            pltpu.roll(first, (LINES + 2) * COLS - 1, 0).astype(BF16),
        ],
        axis=1,
    )
    n_out = LINES * COLS
    spatial = nt(wide[0:n_out], conv_blocks[0])
    spatial = spatial + nt(wide[COLS : COLS + n_out], conv_blocks[1])
    spatial = spatial + nt(wide[2 * COLS : 2 * COLS + n_out], conv_blocks[2])
    spatial = spatial.reshape(LINES, COLS, 128)[:, :SIDE, :].reshape(16 * QUARTER, 128)

    sent_stats += offer(stat2, local_stats(spatial), 1)
    collect(stat2, 1)
    mean, var = whole_stats(stat2, COUNT)
    second = jnp.maximum((spatial - mean) * lax.rsqrt(var + 1e-05) * vec_all[2:3] + vec_all[3:4], 0.0).astype(BF16)
    mid[0:QUARTER] = second.reshape(QUARTER, 16, 128)
    spread(mid, hold2, 0, 1)
    spread(mid, hold2, 1, 1)

    copies3 = []
    for q in range(4):
        stat3s[q] = local_stats(nt(second, diagonal(exp_w[q].astype(F32))))
    for j in range(1, 4):
        q = (mp + j) % 4
        copy = remote(stat3s.at[q], stat3.at[mp], s_send.at[2, j - 1], s_recv.at[2, j - 1], (dp, q))
        copy.start()
        copies3.append(copy)
    stat3[mp] = stat3s[mp]
    sent_stats += copies3
    collect(stat3, 2)
    mean, var = whole_stats(stat3, COUNT)
    mid[QUARTER] = stat_tile(pieces(mean) + pieces(lax.rsqrt(var + 1e-05)))
    spread_stats(mid, hold2, 1)
    permute(hold2, inv, out2, home, 1, holder, held, held_part)

    def a_of(q):
        return second_all.at[pl.ds(QUARTER * q, A_TILES)]

    def b_of(q):
        return second_all.at[pl.ds(QUARTER * q + A_TILES, B_TILES)]

    ag = [
        remote(a_of(mp), a_of(mp), ag_send.at[0], ag_recv.at[0], to_r),
        remote(a_of(mp), a_of(mp), ag_send.at[1], ag_recv.at[1], to_l),
        remote(b_of(mp), b_of(mp), ag_send.at[2], ag_recv.at[2], to_l),
        remote(b_of(mp), b_of(mp), ag_send.at[3], ag_recv.at[3], to_r),
        remote(a_of(left), a_of(left), ag_send.at[4], ag_recv.at[4], to_r),
        remote(b_of(right), b_of(right), ag_send.at[5], ag_recv.at[5], to_l),
    ]
    arrived(home, 1, 0)
    second_all[pl.ds(QUARTER * mp, A_TILES)] = home[0:A_TILES]
    ag[0].start()
    ag[1].start()
    arrived(home, 1, 1)
    second_all[pl.ds(QUARTER * mp + A_TILES, B_TILES)] = home[A_TILES:QUARTER]
    ag[2].start()
    ag[3].start()
    bytes_of(a_of(left), ag_recv.at[0])
    ag[4].start()
    bytes_of(b_of(right), ag_recv.at[2])
    ag[5].start()
    arrived(home, 1, 2)

    identity = jnp.where(
        lax.broadcasted_iota(jnp.int32, (128, 128), 0) == lax.broadcasted_iota(jnp.int32, (128, 128), 1),
        1.0,
        0.0,
    ).astype(BF16)
    columns = nt(identity, home[QUARTER])
    mean_c = columns[:, 0:1] + columns[:, 1:2] + columns[:, 2:3]
    scale_c = columns[:, 3:4] + columns[:, 4:5] + columns[:, 5:6]

    def expand(block, lanes):
        v = nt(we_block, block)
        third = ((v - mean_c) * scale_c * gain_c + shift_c).astype(BF16).astype(F32)
        f = jnp.maximum(third + img[:, lanes].astype(F32), 0.0).astype(BF16)
        feat[:, lanes] = f
        return f.astype(F32)

    def expand_at(i, pooled):
        j = ((QUARTER * far + QUARTER - 1) // 32 + 1 + i) % 6
        block = second_all[pl.ds(32 * j, 32)].reshape(512, 128)
        f = expand(block, pl.ds(pl.multiple_of(512 * j, 512), 512))
        return pooled + (f[:, 0:128] + f[:, 128:256] + f[:, 256:384] + f[:, 384:512])

    bytes_of(a_of(right), ag_recv.at[1])
    bytes_of(b_of(left), ag_recv.at[3])
    pooled = jnp.zeros((128, 128), F32)
    for i in range(3):
        pooled = expand_at(i, pooled)
    bytes_of(a_of(far), ag_recv.at[4])
    bytes_of(b_of(far), ag_recv.at[5])
    for i in range(3, 6):
        pooled = expand_at(i, pooled)
    rest = expand(second_all[192:196].reshape(64, 128), slice(3072, 3136))
    write = pltpu.make_async_copy(feat, feat_hbm, feat_sem)
    write.start()
    pooled = jnp.sum(pooled, axis=1, keepdims=True) + jnp.sum(rest, axis=1, keepdims=True)
    pooled = pooled / float(PIXELS)

    proj2 = jnp.concatenate([proj[...], proj[...]], axis=0).astype(F32)
    terms = pooled * proj2
    e0 = jnp.sum(terms[0:64], axis=0, keepdims=True)
    e1 = jnp.sum(terms[64:128], axis=0, keepdims=True)
    row8 = lax.broadcasted_iota(jnp.int32, (8, 128), 0)
    top = jnp.where(row8 == 0, e0, jnp.where(row8 == 1, e1, 0.0))
    emb[core, mp] = jnp.concatenate([top, mass[0:8]], axis=0)
    mine = emb.at[core, mp]
    e_copies = []
    for j in range(1, 4):
        e_copies.append(remote(mine, mine, e_send.at[j], e_recv.at[j], (dp, (mp + j) % 4)))
    for j in range(4):
        e_copies.append(remote(mine, mine, e_send.at[4 + j], e_recv.at[4 + j], (other, (mp + j) % 4)))
    for copy in e_copies:
        copy.start()
    for j in range(1, 4):
        bytes_of(emb.at[core, (mp + 4 - j) % 4], e_recv.at[j])
    for j in range(4):
        bytes_of(emb.at[1 - core, (mp + 4 - j) % 4], e_recv.at[4 + j])

    key_tile = jnp.zeros((16, 128), F32)
    for cc in range(2):
        e = emb[cc, 0, 0:8] + emb[cc, 1, 0:8] + emb[cc, 2, 0:8] + emb[cc, 3, 0:8]
        key = e * lax.rsqrt(jnp.sum(e * e, axis=1, keepdims=True) + 1e-06)
        for b in range(2):
            here = q_row == 4 * (me % 4) + 2 * cc + b
            key_tile = jnp.where(here, key[b : b + 1], key_tile)
    queue = emb[core, 0, 8:16] + emb[core, 1, 8:16] + emb[core, 2, 8:16] + emb[core, 3, 8:16]
    z = me % 8
    slab = me // 8
    keys1[z] = key_tile.astype(BF16)
    k_copies = []
    for j in range(1, 8):
        h = slab * 8 + (z + j) % 8
        k_copies.append(remote(keys1.at[z], keys1.at[z], k_send.at[0, j], k_recv.at[0, j], (h * 2 + core, mp)))
    for copy in k_copies:
        copy.start()
    for j in range(1, 8):
        bytes_of(keys1.at[(z + 8 - j) % 8], k_recv.at[0, j])
    keys2[slab] = jnp.sum(keys1[...].astype(F32).reshape(2, 4, 16, 128), axis=1).astype(BF16)
    k_copies2 = []
    for j in range(1, 8):
        h = (me + 8 * j) % CHIPS
        k_copies2.append(
            remote(keys2.at[slab], keys2.at[slab], k_send.at[1, j], k_recv.at[1, j], (h * 2 + core, mp))
        )
    for copy in k_copies2:
        copy.start()
    for j in range(1, 8):
        bytes_of(keys2.at[(slab + 8 - j) % 8], k_recv.at[1, j])
    every = keys2[...].reshape(256, 128)
    score = (nt(unit, every) / DIVISOR)[0:8]
    score_out[...] = score[0:2]
    lane = lax.broadcasted_iota(jnp.int32, (8, 256), 1)
    row = lax.broadcasted_iota(jnp.int32, (8, 256), 0)
    matched = jnp.sum(jnp.where(lane == 2 * dp + row, score, 0.0), axis=1, keepdims=True)
    mass_all = jnp.sum(jnp.exp(score), axis=1, keepdims=True) + queue[:, 0:1]
    losses = jnp.broadcast_to(jnp.log(mass_all) - matched, (8, 128))
    lane8 = lax.broadcasted_iota(jnp.int32, (8, 128), 1)
    loss_out[...] = jnp.sum(jnp.where(row8 == lane8, losses, 0.0), axis=0, keepdims=True)[:, 0:2]

    write.wait()
    for copy in rs + sent + sent_stats + ag + halos + e_copies + k_copies + k_copies2:
        copy.wait_send()
    for slot, (src, out) in enumerate(((field, out1), (mid, out2))):

        @pl.when(holder)
        def _():
            bytes_of(src.at[pl.ds(0, BACK - 1)], hop_send.at[slot])
            bytes_of(out.at[pl.ds(0, CHIPS - 1)], out_send.at[slot])

        @pl.when(jnp.logical_not(holder))
        def _():
            bytes_of(src, hop_send.at[slot])


def on_device(
    images,
    permutation,
    inverse,
    reduce_weight,
    reduce_gain,
    reduce_shift,
    spatial_weight,
    spatial_gain,
    spatial_shift,
    expand_weight,
    expand_gain,
    expand_shift,
    projection,
    queries,
    dictionary_bank,
):
    cw = jnp.transpose(spatial_weight, (2, 3, 0, 1))
    rows = [
        v.reshape(1, -1)
        for v in (reduce_gain, reduce_shift, spatial_gain, spatial_shift, expand_gain, expand_shift)
    ]

    vmem = pl.BlockSpec(memory_space=pltpu.VMEM)
    smem = pl.BlockSpec(memory_space=pltpu.SMEM)
    dma = pltpu.SemaphoreType.DMA
    feat, score, loss = pl.pallas_call(
        kernel,
        out_shape=(
            jax.ShapeDtypeStruct((128, PIXELS), BF16),
            jax.ShapeDtypeStruct((2, 256), F32),
            jax.ShapeDtypeStruct((1, 2), F32),
        ),
        in_specs=[smem, smem, pl.BlockSpec(memory_space=pl.ANY)] + [vmem] * 12,
        out_specs=(pl.BlockSpec(memory_space=pl.ANY), vmem, vmem),
        scratch_shapes=[
            pltpu.VMEM((128, PIXELS), BF16),
            pltpu.VMEM((128, PIXELS), BF16),
            pltpu.VMEM((4 * QUARTER, 16, 128), BF16),
            pltpu.VMEM((QUARTER, 16, 128), BF16),
            pltpu.VMEM((QUARTER, 16, 128), BF16),
            pltpu.VMEM((A_TILES, 16, 128), BF16),
            pltpu.VMEM((B_TILES, 16, 128), BF16),
            pltpu.VMEM((A_TILES, 16, 128), BF16),
            pltpu.VMEM((B_TILES, 16, 128), BF16),
            pltpu.VMEM((4, 3, 16, 384), BF16),
            pltpu.VMEM((4, 64, 128), BF16),
            pltpu.VMEM((4, 8, 128), F32),
            pltpu.VMEM((BACK, 16, 128), BF16),
            pltpu.VMEM((CHIPS, 2, 2, 16, 128), BF16),
            pltpu.VMEM((CHIPS, 16, 128), BF16),
            pltpu.VMEM((BACK, 16, 128), BF16),
            pltpu.VMEM((4, 16, 128), F32),
            pltpu.VMEM((4, 16, 128), F32),
            pltpu.VMEM((4, 16, 128), F32),
            pltpu.VMEM((4, 16, 128), F32),
            pltpu.VMEM((BACK, 16, 128), BF16),
            pltpu.VMEM((CHIPS, 2, 2, 16, 128), BF16),
            pltpu.VMEM((CHIPS, 16, 128), BF16),
            pltpu.VMEM((BACK, 16, 128), BF16),
            pltpu.VMEM((4 * QUARTER, 16, 128), BF16),
            pltpu.VMEM((2, 4, 16, 128), F32),
            pltpu.VMEM((8, 16, 128), BF16),
            pltpu.VMEM((8, 2, 16, 128), BF16),
            pltpu.VMEM((4, 16, 128), BF16),
            pltpu.VMEM((4, 16, 128), BF16),
            dma,
            dma,
            dma((6,)),
            dma((6,)),
            dma((3, 3)),
            dma((3, 3)),
            dma((3, 3)),
            dma((3, 3)),
            dma((2,)),
            dma((2, 8)),
            dma((2,)),
            dma((2, 3)),
            dma((2,)),
            dma((2,)),
            dma((2, 8)),
            dma((2, 8)),
            dma((6,)),
            dma((6,)),
            dma((8,)),
            dma((8,)),
            dma((2, 8)),
            dma((2, 8)),
        ],
        compiler_params=pltpu.CompilerParams(
            collective_id=0, has_side_effects=True, vmem_limit_bytes=63 * 1024 * 1024
        ),
        cost_estimate=pl.CostEstimate(
            flops=2 * 3136 * 128 * 128 * 4, bytes_accessed=2 * 128 * 3136 * 2, transcendentals=0
        ),
    )(
        permutation,
        inverse,
        images.reshape(128, PIXELS),
        reduce_weight,
        cw,
        expand_weight,
        *rows,
        projection,
        queries,
        dictionary_bank,
    )
    return feat.reshape(images.shape), score, loss.reshape(2)


def solution(mesh):
    placed = (
        P("dp", "mp", None),
        P(),
        P(),
        P(None, "mp"),
        P("mp"),
        P("mp"),
        P("mp", None, None, None),
        P("mp"),
        P("mp"),
        P("mp", None),
        P("mp"),
        P("mp"),
        P("mp", None),
        P("dp", None),
        P("mp", None),
    )
    return jax.shard_map(
        on_device,
        mesh=mesh,
        in_specs=placed,
        out_specs=(P("dp", "mp", None), P("dp", None), P("dp")),
        check_vma=False,
    )
```

time: 120 us -> 120 us (level)
  Pallas kernels: 114 us -> 116 us
  local copies, waits for them, and re-layouts: 4.74 us -> 3.2 us
    pallas_call x1, Pallas kernels: 114 us -> 116 us  [on_device(): pl.pallas_call(kernel, out_shape=(jax.ShapeDtypeStruct((128, PIXELS), BF1...]
    unnamed x19 -> x7, local copies, waits for them, and re-layouts: 3.71 us -> 3.2 us
where the time goes in v2:
time: 120 us; the launch traced here: 119 us
  Pallas kernels  116 us (97%)
  local copies, waits for them, and re-layouts  3.2 us (3%)
    pallas_call x1, Pallas kernels, on_device(): pl.pallas_call(kernel, out_shape=(jax.ShapeDtypeStruct((128, PIXELS), BF1...  116 us
    unnamed x7, local copies, waits for them, and re-layouts  3.2 us

profile of v2, /device:TPU:1, one launch (start us, length us, event | category | flops | bytes accessed | tf_op | source)
XLA Modules:
  0.0 119.4 jit_solution(13684302074062323878)
XLA Ops:
  0.6 115.6 %shard_map.166 = (bf16[128,3136]{1,0:T(8,128)(2,1)}, f32[2,256]{1,0:T(2,128)}, f32[1,2]{1,0:T(1,128)}) custom-call(s32[256]{0:T(256)} %perm.1, s32[256]{0:T(256)} %inv.1, bf16[128,3136]{1,0:T(8,128)(2,1)} %bitcast.11, bf16[64,64]{1,0:T(8,128)(2,1)} %rw.1, bf16[3,3,16,64]{3,2,1,0:T(8,128)(2,1)} %bitcast.12, bf16[64,64]{1,0:T(8,128)(2,1)} %we.1, ...), custom_call_target="tpu_custom_call" | custom-call | flops 411041792 | bytes 1605632 | tf_op jit(solution)/shard_map/pallas_call | solution.py:689
  116.2 0.0 copy-start
  116.2 2.1 %copy.21 = bf16[2,64,3136]{2,1,0:T(8,128)(2,1)} copy(bf16[2,64,3136]{2,1,0:T(8,128)(2,1)} %bitcast.10) | data formatting | bytes 1605632
  118.3 0.0 copy-done
  118.3 0.0 copy-start.1
  118.3 0.6 copy.22
  118.9 0.0 copy-done.1
  118.9 0.5 copy.23
Async XLA Ops:
  116.2 2.1 %copy-start = (f32[2,256]{1,0:T(2,128)S(1)}, f32[2,256]{1,0:T(2,128)}, u32[]{:S(2)}) copy-start(f32[2,256]{1,0:T(2,128)} %get-tuple-element.13) | copy-start | bytes 6148
  118.3 0.6 copy-start.1

commit v3 on v2

--- a/solution.py
+++ b/solution.py
@@ -17,6 +17,7 @@
 QUARTER = PIXELS // 4 // 16
 A_TILES = 25
 B_TILES = QUARTER - A_TILES
+B_EARLY = 8
 BACK = QUARTER + 1
 STAT_CHIP = CHIPS - 1
 COUNT = 2.0 * (PIXELS // 4)
@@ -178,12 +179,17 @@
     left_b = from_left.at[pl.ds(A_TILES, B_TILES)]
     right_a = from_right.at[pl.ds(0, A_TILES)]
     right_b = from_right.at[pl.ds(A_TILES, B_TILES)]
+    b_first = part.at[pl.ds(QUARTER * right + A_TILES, B_EARLY)]
+    b_later = part.at[pl.ds(QUARTER * right + A_TILES + B_EARLY, B_TILES - B_EARLY)]
+    left_b_first = from_left.at[pl.ds(A_TILES, B_EARLY)]
+    left_b_later = from_left.at[pl.ds(A_TILES + B_EARLY, B_TILES - B_EARLY)]
     rs = [
         remote(a_part(far), via_left, rs_send.at[0], rs_recv.at[0], to_r),
+        remote(b_part(far), via_right, rs_send.at[3], rs_recv.at[3], to_l),
+        remote(b_first, left_b_first, rs_send.at[2], rs_recv.at[2], to_r),
         remote(a_part(left), right_a, rs_send.at[1], rs_recv.at[1], to_l),
-        remote(b_part(right), left_b, rs_send.at[2], rs_recv.at[2], to_r),
-        remote(b_part(far), via_right, rs_send.at[3], rs_recv.at[3], to_l),
         remote(sum_a, left_a, rs_send.at[4], rs_recv.at[4], to_r),
+        remote(b_later, left_b_later, rs_send.at[6], rs_recv.at[6], to_r),
         remote(sum_b, right_b, rs_send.at[5], rs_recv.at[5], to_l),
     ]
     for copy in rs[:4]:
@@ -236,10 +242,11 @@
     own = part[pl.ds(QUARTER * right, A_TILES)].astype(F32)
     sum_a[...] = (own + via_left[...].astype(F32)).astype(BF16)
     rs[4].start()
-    rs[3].wait_recv()
+    rs[5].start()
+    rs[1].wait_recv()
     own = part[pl.ds(QUARTER * left + A_TILES, B_TILES)].astype(F32)
     sum_b[...] = (own + via_right[...].astype(F32)).astype(BF16)
-    rs[5].start()
+    rs[6].start()
 
     sent += share(conv_w, 0)
     sent += share(exp_w, 1)
@@ -307,7 +314,7 @@
             return carry
 
         def take_other(i, carry):
-            g = (me // 8 + 8 - i) % 8
+            g = (me // 8 + 16 - i) % 8
             bytes_of(hold.at[pl.ds(8 * g, 8), 1 - core, 0], pair_recv.at[slot, g])
             turn(1 - core, g)
             return carry
@@ -326,12 +333,12 @@
 
         @pl.when(holds)
         def _():
+            lax.fori_loop(1, 8, take, 0)
             g = me // 8
             bytes_of(hold.at[pl.ds(8 * g, 7), core, 0], hop_recv.at[slot, g])
             swapping(g).start()
             turn(core, g)
-            lax.fori_loop(1, 8, take, 0)
-            lax.fori_loop(0, 8, take_other, 0)
+            lax.fori_loop(1, 9, take_other, 0)
 
             def step(i, carry):
                 ts = [(me + 1 + 9 * i + u) % CHIPS for u in range(9)]
@@ -366,14 +373,14 @@
                 bytes_of(dst.at[pl.ds(start, n - 1)], out_recv.at[slot, part_of])
 
     rs[4].wait_recv()
-    rs[1].wait_recv()
+    rs[3].wait_recv()
     total = part[pl.ds(QUARTER * mp, A_TILES)].astype(F32)
     total = total + left_a[...].astype(F32) + right_a[...].astype(F32)
     field[0:A_TILES] = total.astype(BF16)
     spread(field, hold1, 0, 0)
 
-    rs[2].wait_recv()
-    rs[5].wait_recv()
+    for copy in (rs[2], rs[5], rs[6]):
+        copy.wait_recv()
     total = part[pl.ds(QUARTER * mp + A_TILES, B_TILES)].astype(F32)
     total = total + left_b[...].astype(F32) + right_b[...].astype(F32)
     field[A_TILES:QUARTER] = total.astype(BF16)
@@ -436,6 +443,10 @@
     field[QUARTER] = stat_tile(pieces(mean) + pieces(var))
     spread_stats(field, hold1, 0)
 
+    holder = jnp.logical_or(jnp.logical_or(holds_a, holds_b), holds_s)
+    held = jnp.where(holds_s, QUARTER, jnp.where(holds_a, pair, pair + A_TILES))
+    held_part = jnp.where(holds_s, 2, jnp.where(holds_a, 0, 1))
+    permute(hold1, perm, out1, group, 0, holder, held, held_part)
     for n, buf in enumerate((conv_w, exp_w, vecs)):
         shared(buf, sent, n)
     conv_blocks = []
@@ -443,10 +454,6 @@
         w = jnp.concatenate([conv_w[q, dy] for q in range(4)] * 2, axis=0).astype(F32)
         conv_blocks.append(jnp.where(same, w, 0.0).astype(BF16))
     vec_all = vecs[0] + vecs[1] + vecs[2] + vecs[3]
-    holder = jnp.logical_or(jnp.logical_or(holds_a, holds_b), holds_s)
-    held = jnp.where(holds_s, QUARTER, jnp.where(holds_a, pair, pair + A_TILES))
-    held_part = jnp.where(holds_s, 2, jnp.where(holds_a, 0, 1))
-    permute(hold1, perm, out1, group, 0, holder, held, held_part)
     arrived(group, 0, 0)
     arrived(group, 0, 1)
     halos = [
@@ -536,11 +543,11 @@
     arrived(home, 1, 0)
     second_all[pl.ds(QUARTER * mp, A_TILES)] = home[0:A_TILES]
     ag[0].start()
-    ag[1].start()
     arrived(home, 1, 1)
     second_all[pl.ds(QUARTER * mp + A_TILES, B_TILES)] = home[A_TILES:QUARTER]
     ag[2].start()
     ag[3].start()
+    ag[1].start()
     bytes_of(a_of(left), ag_recv.at[0])
     ag[4].start()
     bytes_of(b_of(right), ag_recv.at[2])
@@ -728,8 +735,8 @@
             pltpu.VMEM((4, 16, 128), BF16),
             dma,
             dma,
-            dma((6,)),
-            dma((6,)),
+            dma((7,)),
+            dma((7,)),
             dma((3, 3)),
             dma((3, 3)),
             dma((3, 3)),

time: 120 us -> 118 us (0.983)
  Pallas kernels: 116 us -> 114 us
    pallas_call x1, Pallas kernels: 116 us -> 114 us  [on_device(): pl.pallas_call(kernel, out_shape=(jax.ShapeDtypeStruct((128, PIXELS), BF1...]
where the time goes in v3:
time: 118 us
  Pallas kernels  114 us (97%)
  local copies, waits for them, and re-layouts  3.2 us (3%)
    pallas_call x1, Pallas kernels, on_device(): pl.pallas_call(kernel, out_shape=(jax.ShapeDtypeStruct((128, PIXELS), BF1...  114 us
    unnamed x7, local copies, waits for them, and re-layouts  3.2 us

profile of v3, /device:TPU:1, one launch (start us, length us, event | category | flops | bytes accessed | tf_op | source)
XLA Modules:
  0.0 117.7 jit_solution(18204900069449717530)
XLA Ops:
  0.6 113.9 %shard_map.166 = (bf16[128,3136]{1,0:T(8,128)(2,1)}, f32[2,256]{1,0:T(2,128)}, f32[1,2]{1,0:T(1,128)}) custom-call(s32[256]{0:T(256)} %perm.1, s32[256]{0:T(256)} %inv.1, bf16[128,3136]{1,0:T(8,128)(2,1)} %bitcast.11, bf16[64,64]{1,0:T(8,128)(2,1)} %rw.1, bf16[3,3,16,64]{3,2,1,0:T(8,128)(2,1)} %bitcast.12, bf16[64,64]{1,0:T(8,128)(2,1)} %we.1, ...), custom_call_target="tpu_custom_call" | custom-call | flops 411041792 | bytes 1605632 | tf_op jit(solution)/shard_map/pallas_call | solution.py:696
  114.5 0.0 copy-start
  114.5 2.1 %copy.21 = bf16[2,64,3136]{2,1,0:T(8,128)(2,1)} copy(bf16[2,64,3136]{2,1,0:T(8,128)(2,1)} %bitcast.10) | data formatting | bytes 1605632
  116.6 0.0 copy-done
  116.6 0.0 copy-start.1
  116.6 0.6 copy.22
  117.2 0.0 copy-done.1
  117.2 0.5 copy.23
Async XLA Ops:
  114.5 2.1 %copy-start = (f32[2,256]{1,0:T(2,128)S(1)}, f32[2,256]{1,0:T(2,128)}, u32[]{:S(2)}) copy-start(f32[2,256]{1,0:T(2,128)} %get-tuple-element.13) | copy-start | bytes 6148
  116.6 0.6 copy-start.1

commit v4 on v3

--- a/solution.py
+++ b/solution.py
@@ -248,15 +248,16 @@
     sum_b[...] = (own + via_right[...].astype(F32)).astype(BF16)
     rs[6].start()
 
-    sent += share(conv_w, 0)
-    sent += share(exp_w, 1)
-    sent += share(vecs, 2)
 
     low = lax.broadcasted_iota(jnp.int32, (16, 128), 1) < 64
     pair = me // 2
     holds_a = jnp.logical_and(me % 2 == 0, pair < A_TILES)
     holds_b = jnp.logical_and(me % 2 == 1, pair < B_TILES)
     holds_s = me == STAT_CHIP
+    holds_data = jnp.logical_or(holds_a, holds_b)
+    holder = jnp.logical_or(holds_data, holds_s)
+    held = jnp.where(holds_s, QUARTER, jnp.where(holds_a, pair, pair + A_TILES))
+    held_part = jnp.where(holds_s, 2, jnp.where(holds_a, 0, 1))
 
     def send_tile(src, t, hold, h, slot):
         remote(
@@ -296,7 +297,7 @@
         def _():
             hold[STAT_CHIP, core, 0] = src[QUARTER]
 
-    def permute(hold, order, out, dst, slot, holds, tile, part_of):
+    def receive(hold, slot, holds):
         def turn(side, g):
             at = pl.ds(8 * g, 8)
             x = hold[at, side, 0].reshape(128, 128).astype(F32)
@@ -322,14 +323,6 @@
         def swapped(i, carry):
             swapping(i).wait_send()
             return carry
-
-        def pick(t):
-            at = 4 * t + 2 * core
-            i0 = order[at]
-            i1 = order[at + 1]
-            x0 = hold[i0 >> 2, (i0 >> 1) & 1, i0 & 1]
-            x1 = hold[i1 >> 2, (i1 >> 1) & 1, 1 - (i1 & 1)]
-            return jnp.where(low, x0, x1)
 
         @pl.when(holds)
         def _():
@@ -339,7 +332,19 @@
             swapping(g).start()
             turn(core, g)
             lax.fori_loop(1, 9, take_other, 0)
-
+            lax.fori_loop(0, 8, swapped, 0)
+
+    def deal(hold, order, out, dst, slot, holds, tile, part_of):
+        def pick(t):
+            at = 4 * t + 2 * core
+            i0 = order[at]
+            i1 = order[at + 1]
+            x0 = hold[i0 >> 2, (i0 >> 1) & 1, i0 & 1]
+            x1 = hold[i1 >> 2, (i1 >> 1) & 1, 1 - (i1 & 1)]
+            return jnp.where(low, x0, x1)
+
+        @pl.when(holds)
+        def _():
             def step(i, carry):
                 ts = [(me + 1 + 9 * i + u) % CHIPS for u in range(9)]
                 values = [pick(t) for t in ts]
@@ -357,7 +362,6 @@
 
             lax.fori_loop(0, 7, step, 0)
             dst[tile] = pick(me)
-            lax.fori_loop(0, 8, swapped, 0)
 
     def arrived(dst, slot, part_of):
         start, n, holds = ((0, A_TILES, holds_a), (A_TILES, B_TILES, holds_b), (QUARTER, 1, holds_s))[part_of]
@@ -431,6 +435,10 @@
     square = jnp.sum(dev * dev, axis=0, keepdims=True)
     tile = jnp.concatenate([jnp.broadcast_to(mean, (8, 128)), jnp.broadcast_to(square, (8, 128))], axis=0)
     sent_stats = offer(stat1, tile, 0)
+    sent += share(conv_w, 0)
+    sent += share(exp_w, 1)
+    sent += share(vecs, 2)
+    receive(hold1, 0, holds_data)
     collect(stat1, 0)
     mean, var = whole_stats(stat1, half_count)
 
@@ -442,11 +450,9 @@
 
     field[QUARTER] = stat_tile(pieces(mean) + pieces(var))
     spread_stats(field, hold1, 0)
-
-    holder = jnp.logical_or(jnp.logical_or(holds_a, holds_b), holds_s)
-    held = jnp.where(holds_s, QUARTER, jnp.where(holds_a, pair, pair + A_TILES))
-    held_part = jnp.where(holds_s, 2, jnp.where(holds_a, 0, 1))
-    permute(hold1, perm, out1, group, 0, holder, held, held_part)
+    receive(hold1, 0, holds_s)
+
+    deal(hold1, perm, out1, group, 0, holder, held, held_part)
     for n, buf in enumerate((conv_w, exp_w, vecs)):
         shared(buf, sent, n)
     conv_blocks = []
@@ -520,11 +526,13 @@
         copies3.append(copy)
     stat3[mp] = stat3s[mp]
     sent_stats += copies3
+    receive(hold2, 1, holds_data)
     collect(stat3, 2)
     mean, var = whole_stats(stat3, COUNT)
     mid[QUARTER] = stat_tile(pieces(mean) + pieces(lax.rsqrt(var + 1e-05)))
     spread_stats(mid, hold2, 1)
-    permute(hold2, inv, out2, home, 1, holder, held, held_part)
+    receive(hold2, 1, holds_s)
+    deal(hold2, inv, out2, home, 1, holder, held, held_part)
 
     def a_of(q):
         return second_all.at[pl.ds(QUARTER * q, A_TILES)]

time: 118 us -> 118 us (level)
  no operation moved by 1% of the time
where the time goes in v4:
time: 118 us
  Pallas kernels  114 us (97%)
  local copies, waits for them, and re-layouts  3.2 us (3%)
    pallas_call x1, Pallas kernels, on_device(): pl.pallas_call(kernel, out_shape=(jax.ShapeDtypeStruct((128, PIXELS), BF1...  114 us
    unnamed x7, local copies, waits for them, and re-layouts  3.2 us

profile of v4, /device:TPU:1, one launch (start us, length us, event | category | flops | bytes accessed | tf_op | source)
XLA Modules:
  0.0 117.8 jit_solution(18237629054338986030)
XLA Ops:
  0.6 114.0 %shard_map.166 = (bf16[128,3136]{1,0:T(8,128)(2,1)}, f32[2,256]{1,0:T(2,128)}, f32[1,2]{1,0:T(1,128)}) custom-call(s32[256]{0:T(256)} %perm.1, s32[256]{0:T(256)} %inv.1, bf16[128,3136]{1,0:T(8,128)(2,1)} %bitcast.11, bf16[64,64]{1,0:T(8,128)(2,1)} %rw.1, bf16[3,3,16,64]{3,2,1,0:T(8,128)(2,1)} %bitcast.12, bf16[64,64]{1,0:T(8,128)(2,1)} %we.1, ...), custom_call_target="tpu_custom_call" | custom-call | flops 411041792 | bytes 1605632 | tf_op jit(solution)/shard_map/pallas_call | solution.py:704
  114.6 0.0 copy-start
  114.6 2.1 %copy.21 = bf16[2,64,3136]{2,1,0:T(8,128)(2,1)} copy(bf16[2,64,3136]{2,1,0:T(8,128)(2,1)} %bitcast.10) | data formatting | bytes 1605632
  116.7 0.0 copy-done
  116.7 0.0 copy-start.1
  116.7 0.6 copy.22
  117.3 0.0 copy-done.1
  117.3 0.5 copy.23
Async XLA Ops:
  114.6 2.1 %copy-start = (f32[2,256]{1,0:T(2,128)S(1)}, f32[2,256]{1,0:T(2,128)}, u32[]{:S(2)}) copy-start(f32[2,256]{1,0:T(2,128)} %get-tuple-element.13) | copy-start | bytes 6148
  116.7 0.6 copy-start.1

commit v5 on v4

--- a/solution.py
+++ b/solution.py
@@ -15,11 +15,12 @@
 CHIPS = 64
 LINES = SIDE // 4
 QUARTER = PIXELS // 4 // 16
-A_TILES = 25
+A_TILES = 24
 B_TILES = QUARTER - A_TILES
 B_EARLY = 8
-BACK = QUARTER + 1
-STAT_CHIP = CHIPS - 1
+A_PAIRS = 12
+DATA_PAIRS = 25
+BACK = DATA_PAIRS + 1
 COUNT = 2.0 * (PIXELS // 4)
 DIVISOR = 0.2
 
@@ -249,59 +250,39 @@
     rs[6].start()
 
 
-    low = lax.broadcasted_iota(jnp.int32, (16, 128), 1) < 64
-    pair = me // 2
-    holds_a = jnp.logical_and(me % 2 == 0, pair < A_TILES)
-    holds_b = jnp.logical_and(me % 2 == 1, pair < B_TILES)
-    holds_s = me == STAT_CHIP
-    holds_data = jnp.logical_or(holds_a, holds_b)
-    holder = jnp.logical_or(holds_data, holds_s)
-    held = jnp.where(holds_s, QUARTER, jnp.where(holds_a, pair, pair + A_TILES))
+    low = lax.broadcasted_iota(jnp.int32, (2, 16, 128), 2) < 64
+    pair = (13 * me) % CHIPS
+    holds_a = pair < A_PAIRS
+    holds_b = jnp.logical_and(pair >= A_PAIRS, pair < DATA_PAIRS)
+    holds_s = pair == DATA_PAIRS
+    holds_data = pair < DATA_PAIRS
+    holder = pair < BACK
     held_part = jnp.where(holds_s, 2, jnp.where(holds_a, 0, 1))
 
-    def send_tile(src, t, hold, h, slot):
-        remote(
-            src.at[t],
-            hold.at[me, core, 0],
-            hop_send.at[slot],
-            hop_recv.at[slot, me // 8],
-            (h * 2 + core, mp),
-        ).start()
-
-    def spread(src, hold, odd, slot):
-        n = B_TILES if odd else A_TILES
-
-        def step(i, carry):
-            for u in range(8):
-                t = (pair + 8 * i + u) % (CHIPS // 2)
-                h = 2 * t + odd
-
-                @pl.when(jnp.logical_and(h != me, t < n))
-                def _():
-                    send_tile(src, t + odd * A_TILES, hold, h, slot)
-
-            return carry
-
-        lax.fori_loop(0, 4, step, 0)
-
-        @pl.when(holds_b if odd else holds_a)
+    def spread(src, hold, slot, first, n):
+        for i in range(n):
+            p = first + (me + i) % n
+            h = (5 * p) % CHIPS
+
+            @pl.when(h != me)
+            def _():
+                remote(
+                    src.at[p],
+                    hold.at[me, core, 0],
+                    hop_send.at[slot],
+                    hop_recv.at[slot, me // 8],
+                    (h * 2 + core, mp),
+                ).start()
+
+        @pl.when(jnp.logical_and(pair >= first, pair < first + n))
         def _():
-            hold[me, core, 0] = src[pair + odd * A_TILES]
-
-    def spread_stats(src, hold, slot):
-        @pl.when(me != STAT_CHIP)
-        def _():
-            send_tile(src, QUARTER, hold, STAT_CHIP, slot)
-
-        @pl.when(holds_s)
-        def _():
-            hold[STAT_CHIP, core, 0] = src[QUARTER]
+            hold[me, core, 0] = src[pair]
 
     def receive(hold, slot, holds):
         def turn(side, g):
             at = pl.ds(8 * g, 8)
-            x = hold[at, side, 0].reshape(128, 128).astype(F32)
-            hold[at, side, 1] = pltpu.roll(x, 64, 1).astype(BF16).reshape(8, 16, 128)
+            x = hold[at, side, 0].reshape(256, 128).astype(F32)
+            hold[at, side, 1] = pltpu.roll(x, 64, 1).astype(BF16).reshape(8, 2, 16, 128)
 
         def swapping(g):
             ref = hold.at[pl.ds(8 * g, 8), core, 0]
@@ -334,7 +315,7 @@
             lax.fori_loop(1, 9, take_other, 0)
             lax.fori_loop(0, 8, swapped, 0)
 
-    def deal(hold, order, out, dst, slot, holds, tile, part_of):
+    def deal(hold, order, out, dst, slot):
         def pick(t):
             at = 4 * t + 2 * core
             i0 = order[at]
@@ -343,7 +324,7 @@
             x1 = hold[i1 >> 2, (i1 >> 1) & 1, 1 - (i1 & 1)]
             return jnp.where(low, x0, x1)
 
-        @pl.when(holds)
+        @pl.when(holder)
         def _():
             def step(i, carry):
                 ts = [(me + 1 + 9 * i + u) % CHIPS for u in range(9)]
@@ -353,18 +334,22 @@
                 for t in ts:
                     remote(
                         out.at[t],
-                        dst.at[tile],
+                        dst.at[pair],
                         out_send.at[slot],
-                        out_recv.at[slot, part_of],
+                        out_recv.at[slot, held_part],
                         (t * 2 + core, mp),
                     ).start()
                 return carry
 
             lax.fori_loop(0, 7, step, 0)
-            dst[tile] = pick(me)
+            dst[pair] = pick(me)
 
     def arrived(dst, slot, part_of):
-        start, n, holds = ((0, A_TILES, holds_a), (A_TILES, B_TILES, holds_b), (QUARTER, 1, holds_s))[part_of]
+        start, n, holds = (
+            (0, A_PAIRS, holds_a),
+            (A_PAIRS, DATA_PAIRS - A_PAIRS, holds_b),
+            (DATA_PAIRS, 1, holds_s),
+        )[part_of]
 
         @pl.when(jnp.logical_not(holds))
         def _():
@@ -380,15 +365,16 @@
     rs[3].wait_recv()
     total = part[pl.ds(QUARTER * mp, A_TILES)].astype(F32)
     total = total + left_a[...].astype(F32) + right_a[...].astype(F32)
-    field[0:A_TILES] = total.astype(BF16)
-    spread(field, hold1, 0, 0)
+    field[0:A_PAIRS] = total.astype(BF16).reshape(A_PAIRS, 2, 16, 128)
+    spread(field, hold1, 0, 0, A_PAIRS)
 
     for copy in (rs[2], rs[5], rs[6]):
         copy.wait_recv()
     total = part[pl.ds(QUARTER * mp + A_TILES, B_TILES)].astype(F32)
     total = total + left_b[...].astype(F32) + right_b[...].astype(F32)
-    field[A_TILES:QUARTER] = total.astype(BF16)
-    spread(field, hold1, 1, 0)
+    total = jnp.concatenate([total, jnp.zeros((1, 16, 128), F32)], axis=0)
+    field[A_PAIRS:DATA_PAIRS] = total.astype(BF16).reshape(DATA_PAIRS - A_PAIRS, 2, 16, 128)
+    spread(field, hold1, 0, A_PAIRS, DATA_PAIRS - A_PAIRS)
 
     def both(x):
         x = jnp.broadcast_to(x, (8, 128))
@@ -428,7 +414,7 @@
         b = (v - a).astype(BF16).astype(F32)
         return [a, b, v - a - b]
 
-    x = field[0:QUARTER].reshape(16 * QUARTER, 128).astype(F32)
+    x = field[0:DATA_PAIRS].reshape(32 * DATA_PAIRS, 128)[0 : 16 * QUARTER].astype(F32)
     half_count = COUNT / 2.0
     mean = jnp.sum(x, axis=0, keepdims=True) / half_count
     dev = x - mean
@@ -446,13 +432,13 @@
         tile = jnp.zeros((16, 128), F32)
         for r, v in enumerate(values):
             tile = jnp.where(q_row == r, v, tile)
-        return tile.astype(BF16)
-
-    field[QUARTER] = stat_tile(pieces(mean) + pieces(var))
-    spread_stats(field, hold1, 0)
+        return jnp.concatenate([tile, jnp.zeros((16, 128), F32)], axis=0).astype(BF16).reshape(2, 16, 128)
+
+    field[DATA_PAIRS] = stat_tile(pieces(mean) + pieces(var))
+    spread(field, hold1, 0, DATA_PAIRS, 1)
     receive(hold1, 0, holds_s)
 
-    deal(hold1, perm, out1, group, 0, holder, held, held_part)
+    deal(hold1, perm, out1, group, 0)
     for n, buf in enumerate((conv_w, exp_w, vecs)):
         shared(buf, sent, n)
     conv_blocks = []
@@ -463,15 +449,15 @@
     arrived(group, 0, 0)
     arrived(group, 0, 1)
     halos = [
-        remote(group.at[pl.ds(0, 4)], halo_bottom, halo_send.at[0], halo_recv.at[0], to_l),
-        remote(group.at[pl.ds(QUARTER - 4, 4)], halo_top, halo_send.at[1], halo_recv.at[1], to_r),
+        remote(group.at[pl.ds(0, 2)], halo_bottom, halo_send.at[0], halo_recv.at[0], to_l),
+        remote(group.at[pl.ds(DATA_PAIRS - 3, 3)], halo_top, halo_send.at[1], halo_recv.at[1], to_r),
     ]
     for copy in halos:
         copy.start()
     arrived(group, 0, 2)
 
 
-    marks = group[QUARTER].astype(F32)
+    marks = group[DATA_PAIRS, 0].astype(F32)
     mean_i = marks[0:1] + marks[1:2] + marks[2:3]
     var_i = marks[3:4] + marks[4:5] + marks[5:6]
     mean = (both(mean_i) * 0.5)[0:1]
@@ -480,14 +466,14 @@
     scale = lax.rsqrt(var + 1e-05)
 
     def norm1(tiles):
-        x = tiles.reshape(-1, 128).astype(F32)
+        x = tiles.astype(F32)
         return jnp.maximum((x - mean) * scale * vec_all[0:1] + vec_all[1:2], 0.0)
 
-    inner = norm1(group[0:QUARTER]).reshape(LINES, SIDE, 128)
+    inner = norm1(group[0:DATA_PAIRS].reshape(32 * DATA_PAIRS, 128)[0 : 16 * QUARTER]).reshape(LINES, SIDE, 128)
     for copy in halos:
         copy.wait_recv()
-    top = norm1(halo_top[...])[8:64]
-    bottom = norm1(halo_bottom[...])[0:SIDE]
+    top = norm1(halo_top[...].reshape(96, 128))[24:80]
+    bottom = norm1(halo_bottom[...].reshape(64, 128))[0:SIDE]
     top = jnp.where(jnp.full((SIDE, 128), mp, jnp.int32) == 0, 0.0, top).reshape(1, SIDE, 128)
     bottom = jnp.where(jnp.full((SIDE, 128), mp, jnp.int32) == 3, 0.0, bottom).reshape(1, SIDE, 128)
     first = jnp.concatenate([top, inner, bottom], axis=0)
@@ -512,9 +498,9 @@
     collect(stat2, 1)
     mean, var = whole_stats(stat2, COUNT)
     second = jnp.maximum((spatial - mean) * lax.rsqrt(var + 1e-05) * vec_all[2:3] + vec_all[3:4], 0.0).astype(BF16)
-    mid[0:QUARTER] = second.reshape(QUARTER, 16, 128)
-    spread(mid, hold2, 0, 1)
-    spread(mid, hold2, 1, 1)
+    padded = jnp.concatenate([second, jnp.zeros((16, 128), BF16)], axis=0)
+    mid[0:DATA_PAIRS] = padded.reshape(DATA_PAIRS, 2, 16, 128)
+    spread(mid, hold2, 1, 0, DATA_PAIRS)
 
     copies3 = []
     for q in range(4):
@@ -529,10 +515,10 @@
     receive(hold2, 1, holds_data)
     collect(stat3, 2)
     mean, var = whole_stats(stat3, COUNT)
-    mid[QUARTER] = stat_tile(pieces(mean) + pieces(lax.rsqrt(var + 1e-05)))
-    spread_stats(mid, hold2, 1)
+    mid[DATA_PAIRS] = stat_tile(pieces(mean) + pieces(lax.rsqrt(var + 1e-05)))
+    spread(mid, hold2, 1, DATA_PAIRS, 1)
     receive(hold2, 1, holds_s)
-    deal(hold2, inv, out2, home, 1, holder, held, held_part)
+    deal(hold2, inv, out2, home, 1)
 
     def a_of(q):
         return second_all.at[pl.ds(QUARTER * q, A_TILES)]
@@ -549,10 +535,10 @@
         remote(b_of(right), b_of(right), ag_send.at[5], ag_recv.at[5], to_l),
     ]
     arrived(home, 1, 0)
-    second_all[pl.ds(QUARTER * mp, A_TILES)] = home[0:A_TILES]
+    second_all[pl.ds(QUARTER * mp, A_TILES)] = home[0:A_PAIRS].reshape(A_TILES, 16, 128)
     ag[0].start()
     arrived(home, 1, 1)
-    second_all[pl.ds(QUARTER * mp + A_TILES, B_TILES)] = home[A_TILES:QUARTER]
+    second_all[pl.ds(QUARTER * mp + A_TILES, B_TILES)] = home[A_PAIRS:DATA_PAIRS].reshape(B_TILES + 1, 16, 128)[0:B_TILES]
     ag[2].start()
     ag[3].start()
     ag[1].start()
@@ -567,7 +553,7 @@
         1.0,
         0.0,
     ).astype(BF16)
-    columns = nt(identity, home[QUARTER])
+    columns = nt(identity, home[DATA_PAIRS, 0])
     mean_c = columns[:, 0:1] + columns[:, 1:2] + columns[:, 2:3]
     scale_c = columns[:, 3:4] + columns[:, 4:5] + columns[:, 5:6]
 
@@ -723,24 +709,24 @@
             pltpu.VMEM((4, 3, 16, 384), BF16),
             pltpu.VMEM((4, 64, 128), BF16),
             pltpu.VMEM((4, 8, 128), F32),
-            pltpu.VMEM((BACK, 16, 128), BF16),
-            pltpu.VMEM((CHIPS, 2, 2, 16, 128), BF16),
-            pltpu.VMEM((CHIPS, 16, 128), BF16),
-            pltpu.VMEM((BACK, 16, 128), BF16),
+            pltpu.VMEM((BACK, 2, 16, 128), BF16),
+            pltpu.VMEM((CHIPS, 2, 2, 2, 16, 128), BF16),
+            pltpu.VMEM((CHIPS, 2, 16, 128), BF16),
+            pltpu.VMEM((BACK, 2, 16, 128), BF16),
             pltpu.VMEM((4, 16, 128), F32),
             pltpu.VMEM((4, 16, 128), F32),
             pltpu.VMEM((4, 16, 128), F32),
             pltpu.VMEM((4, 16, 128), F32),
-            pltpu.VMEM((BACK, 16, 128), BF16),
-            pltpu.VMEM((CHIPS, 2, 2, 16, 128), BF16),
-            pltpu.VMEM((CHIPS, 16, 128), BF16),
-            pltpu.VMEM((BACK, 16, 128), BF16),
+            pltpu.VMEM((BACK, 2, 16, 128), BF16),
+            pltpu.VMEM((CHIPS, 2, 2, 2, 16, 128), BF16),
+            pltpu.VMEM((CHIPS, 2, 16, 128), BF16),
+            pltpu.VMEM((BACK, 2, 16, 128), BF16),
             pltpu.VMEM((4 * QUARTER, 16, 128), BF16),
             pltpu.VMEM((2, 4, 16, 128), F32),
             pltpu.VMEM((8, 16, 128), BF16),
             pltpu.VMEM((8, 2, 16, 128), BF16),
-            pltpu.VMEM((4, 16, 128), BF16),
-            pltpu.VMEM((4, 16, 128), BF16),
+            pltpu.VMEM((3, 2, 16, 128), BF16),
+            pltpu.VMEM((2, 2, 16, 128), BF16),
             dma,
             dma,
             dma((7,)),

time: 118 us -> 123 us (1.042)
  Pallas kernels: 114 us -> 119 us
    pallas_call x1, Pallas kernels: 114 us -> 119 us  [on_device(): pl.pallas_call(kernel, out_shape=(jax.ShapeDtypeStruct((128, PIXELS), BF1...]
where the time goes in v5:
time: 123 us
  Pallas kernels  119 us (97%)
  local copies, waits for them, and re-layouts  3.2 us (3%)
    pallas_call x1, Pallas kernels, on_device(): pl.pallas_call(kernel, out_shape=(jax.ShapeDtypeStruct((128, PIXELS), BF1...  119 us
    unnamed x7, local copies, waits for them, and re-layouts  3.2 us

profile of v5, /device:TPU:1, one launch (start us, length us, event | category | flops | bytes accessed | tf_op | source)
XLA Modules:
  0.0 122.9 jit_solution(16469117479514996654)
XLA Ops:
  0.6 119.1 %shard_map.166 = (bf16[128,3136]{1,0:T(8,128)(2,1)}, f32[2,256]{1,0:T(2,128)}, f32[1,2]{1,0:T(1,128)}) custom-call(s32[256]{0:T(256)} %perm.1, s32[256]{0:T(256)} %inv.1, bf16[128,3136]{1,0:T(8,128)(2,1)} %bitcast.11, bf16[64,64]{1,0:T(8,128)(2,1)} %rw.1, bf16[3,3,16,64]{3,2,1,0:T(8,128)(2,1)} %bitcast.12, bf16[64,64]{1,0:T(8,128)(2,1)} %we.1, ...), custom_call_target="tpu_custom_call" | custom-call | flops 411041792 | bytes 1605632 | tf_op jit(solution)/shard_map/pallas_call | solution.py:690
  119.7 0.0 copy-start
  119.7 2.1 %copy.21 = bf16[2,64,3136]{2,1,0:T(8,128)(2,1)} copy(bf16[2,64,3136]{2,1,0:T(8,128)(2,1)} %bitcast.10) | data formatting | bytes 1605632
  121.8 0.0 copy-done
  121.8 0.0 copy-start.1
  121.8 0.6 copy.22
  122.4 0.0 copy-done.1
  122.4 0.5 copy.23
Async XLA Ops:
  119.7 2.1 %copy-start = (f32[2,256]{1,0:T(2,128)S(1)}, f32[2,256]{1,0:T(2,128)}, u32[]{:S(2)}) copy-start(f32[2,256]{1,0:T(2,128)} %get-tuple-element.13) | copy-start | bytes 6148
  121.8 0.6 copy-start.1
